TPU v7x, 32 devices: a whole 2x2x4 slice. The times are simulated.
32 devices in a mesh: dp: 8 (over y, x, core), shard: 4 (over z).
Axes of the slice: x: 2, y: 2, z: 4, core: 2. Of those that a mesh axis runs over, the one named last changes fastest.
Arguments:
- queries: bfloat16 [4096, 2048], P(('dp', 'shard')), may hold values from -6 to 6
- keys_in: bfloat16 [4096, 2048], P(('dp', 'shard')), may hold values from -6 to 6
- values: bfloat16 [4096, 2048], P(('dp', 'shard')), may hold values from -6 to 6
- out_grad: bfloat16 [4096, 2048], P(('dp', 'shard')), may hold values from -48 to 48
- out_weight: bfloat16 [2048, 2048], P('shard'), may hold values from -0.125 to 0.125
- block_lists: int32 [8, 4, 4], P('dp'), may hold values from 0 to 3, as said below
- voxel_count: int32 [8], P('dp'), may hold values from 256 to 512
Outputs:
- grad_query: bfloat16 [4096, 2048], P(('dp', 'shard'))
- grad_key: bfloat16 [4096, 2048], P(('dp', 'shard'))
- grad_value: bfloat16 [4096, 2048], P(('dp', 'shard'))
- grad_weight: bfloat16 [2048, 2048], P('shard')
Inputs may be any that keep to these rules, and one draw needn't show every extreme that they name: `block_lists`: entry 0 of row b of a scene's list is b itself; the 4 entries of a row are different blocks of that scene.
All inputs are finite; a program needn't handle non-finite values.
Results may differ from a plain program's by a relative error of at most 0.0095.
Values may be sent and summed in bfloat16 or wider, within the bound.
No kernel may reach another device: no remote copies, remote signals or barrier semaphores. Data moves between devices by JAX's collectives and lax.ppermute only.
A program may use at most 128 MiB of HBM per device.

v0:
```python
import functools
import math

import jax
import jax.numpy as jnp
from jax import lax
from jax.experimental import pallas as pl
from jax.experimental.pallas import tpu as pltpu
from jax.sharding import PartitionSpec as P

HDIM = 128
BLOCK = 128
NB = 4
MIB = 1024 * 1024
DP = ("chips", "core")

Z, COUNT, CORE, CHIP = range(4)

EARLY = 3

NO_COST = pl.CostEstimate(flops=0, bytes_accessed=1024, transcendentals=0)

f32 = jnp.float32
bf16 = jnp.bfloat16


def dot(a, b, ca, cb):
    return lax.dot_general(a, b, (((ca,), (cb,)), ((), ())), preferred_element_type=f32)


def sds(shape, dtype):
    return jax.ShapeDtypeStruct(shape, dtype)


def params(mib=2):
    return pltpu.CompilerParams(vmem_limit_bytes=mib * MIB)


def swap(x, axis, size, flip):
    return lax.ppermute(x, axis, [(i, i ^ flip) for i in range(size)])


def after(x, *earlier):
    return lax.optimization_barrier((x, *earlier))[0]


def run_all(copies):
    for copy in copies:
        copy.start()
    for copy in copies:
        copy.wait()


def whole(kernel, out_shape, operands, name, scalars=0, mib=2, scratch=()):
    return pl.pallas_call(
        kernel,
        out_shape=out_shape,
        in_specs=[pl.BlockSpec(memory_space=pltpu.SMEM)] * scalars
        + [pl.BlockSpec(memory_space=pltpu.VMEM)] * (len(operands) - scalars),
        out_specs=jax.tree.map(lambda _: pl.BlockSpec(memory_space=pltpu.VMEM), out_shape),
        scratch_shapes=scratch,
        compiler_params=params(mib),
        cost_estimate=NO_COST,
        name=name,
    )(*operands)


def pack_kernel(meta, q_ref, k_ref, v_ref, grad_ref, mine_ref, *refs):
    *outs, sems = refs
    width = outs[0].shape[2]
    copies = [pltpu.make_async_copy(grad_ref, mine_ref, sems.at[3 * len(outs)])]
    for n, out_ref in enumerate(outs):
        k, first = (n, 0) if n < 2 else (n // 2 + 1, n % 2 * EARLY * HDIM)
        start = pl.multiple_of((meta[Z] ^ k) * width + first, 128)
        for i, ref in enumerate((q_ref, k_ref, v_ref)):
            part = ref.at[:, pl.ds(start, out_ref.shape[2])]
            copies.append(pltpu.make_async_copy(part, out_ref.at[i], sems.at[3 * n + i]))
    run_all(copies)


def pack(meta, queries, keys_in, values, grad):
    rows, width = queries.shape
    part, early = width // 4, EARLY * HDIM
    shapes = [sds((3, rows, n), bf16) for n in (part, part, early, part - early, early, part - early)]
    shapes = [sds(grad.shape, bf16)] + shapes
    return pl.pallas_call(
        pack_kernel,
        out_shape=shapes,
        in_specs=[pl.BlockSpec(memory_space=pltpu.SMEM)] + [pl.BlockSpec(memory_space=pl.ANY)] * 4,
        out_specs=[pl.BlockSpec(memory_space=pltpu.VMEM)] * len(shapes),
        scratch_shapes=[pltpu.SemaphoreType.DMA((3 * len(shapes),))],
        compiler_params=params(),
        cost_estimate=NO_COST,
        name="pack_heads",
    )(meta, queries, keys_in, values, grad)


def token_pos(shape, dim, z, start=0):
    return (lax.broadcasted_iota(jnp.int32, shape, dim) + start) ^ (z * BLOCK)


def grad_attn_kernel(start, meta, *refs):
    *grads, w_ref, out_ref = refs
    grad = jnp.concatenate([g[...] for g in grads], axis=0)
    live = token_pos((grad.shape[0], 1), 0, meta[Z], start) < meta[COUNT]
    tile = 2 * HDIM

    @pl.loop(0, w_ref.shape[0] // tile)
    def _(i):
        part = pl.ds(pl.multiple_of(i * tile, tile), tile)
        out_ref[:, part] = jnp.where(live, dot(grad, w_ref[part, :], 1, 1), 0.0).astype(bf16)


def grad_attn(meta, grads, weight, start):
    shape = (sum(g.shape[0] for g in grads), weight.shape[0])
    kernel = functools.partial(grad_attn_kernel, start)
    return whole(kernel, sds(shape, bf16), (meta, *grads, weight), "grad_attn", 1, 6)


def head_of(pieces, group, h):
    part = pieces[-1].shape[2]
    parts = []
    for p in pieces:
        start = (group * EARLY * HDIM if p.shape[2] > part else 0) + h * HDIM
        parts.append([p[i, :, start : start + HDIM] for i in range(3)])
    return (jnp.concatenate(x, axis=0) for x in zip(*parts))


def forward_kernel(group, meta, p0, p1, p2, p3, weight_ref, inverse_ref, out_ref, heads_ref, bias_ref):
    pieces = (p0, p1, p2, p3)
    rows = p0.shape[1]
    total = 4 * rows
    tile = 2 * rows
    to_power = math.log2(math.e) / math.sqrt(HDIM)
    query_live = token_pos((1, total), 1, meta[Z]) < meta[COUNT]
    key_live = token_pos((total, 1), 0, meta[Z]) < meta[COUNT]
    bias_ref[...] = jnp.where(key_live | ~query_live, 0.0, -jnp.inf)
    for h in range(p3.shape[2] // HDIM):
        cols = slice(h * HDIM, (h + 1) * HDIM)
        query, key, value = head_of(pieces, group, h)
        for t in range(2):
            part = slice(t * tile, (t + 1) * tile)
            scores = dot(key, query[part], 1, 1) + bias_ref[:, part]
            peak = jnp.max(scores, axis=0, keepdims=True)
            weights = jnp.exp2((scores - peak) * to_power).astype(bf16)
            weight_ref[h, :, part] = weights
            inverse = 1.0 / jnp.sum(weights.astype(f32), axis=0, keepdims=True)
            inverse_ref[h, :, part] = inverse
            heads = dot(value, weights, 0, 0) * inverse
            out_ref[cols, part] = heads
            heads_ref[cols, part] = jnp.where(query_live[:, part], heads, 0.0).astype(bf16)


def forward(meta, pieces, group):
    _, rows, width = pieces[-1].shape
    total = 4 * rows
    shapes = [
        sds((width // HDIM, total, total), bf16),
        sds((width // HDIM, 1, total), f32),
        sds((width, total), f32),
        sds((width, total), bf16),
    ]
    scratch = [pltpu.VMEM((total, total), f32)]
    kernel = functools.partial(forward_kernel, group)
    return whole(kernel, shapes, (meta, *pieces), "attend_forward", 1, 8, scratch)


def backward_kernel(meta, own, near, far2a, far3a, far2b, far3b, early_ref, late_ref, *refs):
    saved, back_ref, backs = (refs[:3], refs[3:6]), refs[6], refs[7:]
    rows = own.shape[1]
    total = 4 * rows
    tile = 2 * rows
    scale = 1.0 / math.sqrt(HDIM)
    for n in range(own.shape[2] // HDIM):
        group, h = divmod(n, EARLY)
        query, key, value = head_of(((own, near, far2a, far3a), (own, near, far2b, far3b))[group], group, h)
        weight_ref, inverse_ref, out_ref = saved[group]
        here = slice(h * HDIM, (h + 1) * HDIM)
        cols = slice(n * HDIM, (n + 1) * HDIM)
        grad = jnp.concatenate([early_ref[:, cols], late_ref[:, cols]], axis=0)
        grad_key = grad_value = jnp.zeros((total, HDIM), f32)
        for t in range(2):
            span = slice(t * tile, (t + 1) * tile)
            weights = weight_ref[h, :, span]
            inverse = inverse_ref[h, :, span]
            turned = grad[span].astype(f32).T
            row_delta = jnp.sum(out_ref[here, span] * turned, axis=0, keepdims=True)
            grad_prob = dot(value, grad[span], 1, 1)
            dscore = (weights.astype(f32) * ((grad_prob - row_delta) * (inverse * scale))).astype(bf16)
            grad_query = dot(key, dscore, 0, 0).T.astype(bf16)
            backs[2 * t][0, :, cols] = grad_query[:rows]
            backs[2 * t + 1][0, :, cols] = grad_query[rows:]
            grad_key += dot(dscore, query[span], 1, 0)
            grad_value += dot(weights, (turned * inverse).T.astype(bf16), 1, 0)
        for k in range(4):
            mine = slice(k * rows, (k + 1) * rows)
            backs[k][1, :, cols] = grad_key[mine].astype(bf16)
            backs[k][2, :, cols] = grad_value[mine].astype(bf16)
    for k, ref in enumerate(backs):
        back_ref[meta[Z] ^ k] = ref[...]


def backward(meta, pieces, grads, saved):
    shape = sds((4, *pieces[0].shape), bf16)
    scratch = [pltpu.VMEM(pieces[0].shape, bf16)] * 4
    return whole(backward_kernel, shape, (meta, *pieces, *grads, *saved), "attend_backward", 1, 8, scratch)


LINE = HDIM // 8


def line_at(meta, head, other, j):
    at = head * HDIM + ((meta[CORE] ^ other) * 4 + (meta[CHIP] ^ j)) * LINE
    return pl.ds(pl.multiple_of(at, LINE), LINE)


def weight_kernel(meta, heads_a, heads_b, *refs):
    *grads, send_ref, keep_ref = refs
    width = heads_a.shape[0] + heads_b.shape[0]
    lines = []
    for other in (1, 0):
        for j in range(4):
            for ref in (heads_a, heads_b):
                lines += [ref[line_at(meta, h, other, j), :] for h in range(ref.shape[0] // HDIM)]
    lines = jnp.concatenate(lines, axis=0)
    tile = 4 * HDIM

    @pl.loop(0, send_ref.shape[1] // tile)
    def _(i):
        part = pl.ds(pl.multiple_of(i * tile, tile), tile)
        product = dot(lines, jnp.concatenate([g[:, part] for g in grads], axis=0), 1, 0)
        send_ref[:, part] = product[: width // 2].astype(bf16)
        keep_ref[:, part] = product[width // 2 :]


def weight_halves(meta, heads, grads):
    shape = (sum(x.shape[0] for x in heads) // 2, grads[0].shape[1])
    return whole(weight_kernel, [sds(shape, bf16), sds(shape, f32)], (meta, *heads, *grads), "weight_halves", 1, 6)


def add_kernel(keep_ref, recv_ref, *outs):
    size = outs[0].shape[0]
    for j, out_ref in enumerate(outs):
        part = slice(j * size, (j + 1) * size)
        out_ref[...] = (keep_ref[part, :] + recv_ref[part, :].astype(f32)).astype(out_ref.dtype)


def add_parts(keep, recv):
    shape = (keep.shape[0] // 4, keep.shape[1])
    return whole(add_kernel, [sds(shape, f32)] + [sds(shape, bf16)] * 3, (keep, recv), "add_parts")


def total_kernel(scale, own_ref, r1, r2, r3, out_ref):
    total = own_ref[...] + r1[...].astype(f32) + r2[...].astype(f32) + r3[...].astype(f32)
    out_ref[...] = (total * scale).astype(bf16)


def total_of(own, recvs, scale):
    return whole(functools.partial(total_kernel, scale), sds(own.shape, bf16), (own, *recvs), "scene_mean")


def join_weight_kernel(meta, *refs):
    *parts, out_ref, sems = refs
    copies = []
    for n, ref in enumerate(parts):
        for h in range(ref.shape[0] // LINE):
            line = out_ref.at[line_at(meta, h, n // 4, n % 4), :]
            part = ref.at[pl.ds(h * LINE, LINE), :]
            copies.append(pltpu.make_async_copy(part, line, sems.at[len(copies)]))
    run_all(copies)


def join_weight(meta, parts):
    size, outw = parts[0].shape
    return pl.pallas_call(
        join_weight_kernel,
        out_shape=sds((8 * size, outw), bf16),
        in_specs=[pl.BlockSpec(memory_space=pltpu.SMEM)] + [pl.BlockSpec(memory_space=pltpu.VMEM)] * 8,
        out_specs=pl.BlockSpec(memory_space=pl.ANY),
        scratch_shapes=[pltpu.SemaphoreType.DMA((8 * size // LINE,))],
        compiler_params=params(),
        cost_estimate=NO_COST,
        name="join_weight",
    )(meta, *parts)


def join_kernel(back_ref, *refs):
    *outs, sems = refs
    width = back_ref.shape[3]
    copies = []
    for j in range(4):
        for i, out_ref in enumerate(outs):
            cols = out_ref.at[:, pl.ds(j * width, width)]
            copies.append(pltpu.make_async_copy(back_ref.at[j, i], cols, sems.at[len(copies)]))
    run_all(copies)


def join(back):
    _, _, rows, width = back.shape
    return pl.pallas_call(
        join_kernel,
        out_shape=[sds((rows, 4 * width), bf16)] * 3,
        in_specs=[pl.BlockSpec(memory_space=pltpu.VMEM)],
        out_specs=[pl.BlockSpec(memory_space=pl.ANY)] * 3,
        scratch_shapes=[pltpu.SemaphoreType.DMA((12,))],
        compiler_params=params(),
        cost_estimate=NO_COST,
        name="join_heads",
    )(back)


def dense_body(queries, keys_in, values, out_grad, out_weight, voxel_count):
    meta = jnp.stack([lax.axis_index("shard"), voxel_count[0], lax.axis_index("core"), lax.axis_index("chips")])
    meta = meta.astype(jnp.int32)

    def send(x, k, *earlier):
        return swap(after(x, *earlier) if earlier else x, "shard", 4, k)

    across = send(out_grad, 2)
    beside = send(out_grad, 1)
    mine, own, near1, far2a, far2b, far3a, far3b = pack(meta, queries, keys_in, values, out_grad)
    piece1 = send(near1, 1)
    piece3a = send(far3a, 3, beside)
    piece2a = send(far2a, 2, across)
    piece3b = send(far3b, 3, piece3a)
    piece2b = send(far2b, 2, piece2a)
    half = across.shape[0] // 2
    grad_early = grad_attn(meta, (mine, beside, across), out_weight, 0)
    corners = [send(across[:half], 1), send(after(across, piece1, grad_early)[half:], 1)]

    *saved_a, heads_a = forward(meta, (own, piece1, piece2a, piece3a), 0)
    heads_a, piece2b, piece3b = lax.optimization_barrier((heads_a, piece2b, piece3b))
    *saved_b, heads_b = forward(meta, (own, piece1, piece2b, piece3b), 1)
    grad_early, heads_b, *corners = lax.optimization_barrier((grad_early, heads_b, *corners))
    grads = (mine, beside, across, *corners)

    out, keep = weight_halves(meta, (heads_a, heads_b), grads)
    recv = swap(out, "core", 2, 1)
    grad_late = grad_attn(meta, after(grads[3:], out), out_weight, 3 * BLOCK)
    pieces = (own, piece1, piece2a, piece3a, piece2b, piece3b)
    back = backward(meta, pieces, (grad_early, grad_late), (*saved_a, *saved_b))
    back_all = lax.all_to_all(after(back, recv), "shard", split_axis=0, concat_axis=0, tiled=True)

    own_part, *sends = add_parts(after(keep, back), recv)
    recvs = [swap(x, "chips", 4, j + 1) for j, x in enumerate(sends)]
    done = total_of(own_part, recvs, 1.0 / 8)
    near = [done] + [swap(done, "chips", 4, j) for j in (1, 2, 3)]
    far = [swap(x, "core", 2, 1) for x in near]
    grads_in = join(back_all)
    far[-1] = after(far[-1], grads_in[0])
    return (*grads_in, join_weight(meta, near + far))


def attend_listed(queries, keys_in, values, block_ids, live_count):
    row_count, width_all = queries.shape
    head_count = width_all // HDIM
    block_count = row_count // BLOCK
    score_scale = 1.0 / math.sqrt(HDIM)
    query_blk = queries.reshape(block_count, BLOCK, head_count, HDIM)
    key_blk = keys_in.reshape(block_count, BLOCK, head_count, HDIM)[block_ids].reshape(
        block_count, NB * BLOCK, head_count, HDIM
    )
    value_blk = values.reshape(block_count, BLOCK, head_count, HDIM)[block_ids].reshape(
        block_count, NB * BLOCK, head_count, HDIM
    )
    query_pos = jnp.arange(row_count, dtype=jnp.int32).reshape(block_count, BLOCK)
    key_pos = (
        block_ids[:, :, None] * BLOCK + jnp.arange(BLOCK, dtype=jnp.int32)[None, None, :]
    ).reshape(block_count, NB * BLOCK)
    allowed = (key_pos[:, None, :] < live_count) | (query_pos[:, :, None] >= live_count)
    scores = (
        jnp.einsum("bqhd,bkhd->bhqk", query_blk, key_blk, preferred_element_type=jnp.float32)
        * score_scale
    )
    scores = jnp.where(allowed[:, None], scores, -jnp.inf)
    peak = jnp.max(scores, axis=-1, keepdims=True)
    weights = jnp.exp(scores - peak)
    probs = weights / jnp.sum(weights, axis=-1, keepdims=True)
    return (query_blk, key_blk, value_blk, probs)


def listed_body(queries, keys_in, values, out_grad, out_weight, block_lists, voxel_count):
    local_rows = queries.shape[0]
    live_count = voxel_count[0]
    block_ids = block_lists[0]
    positions = lax.axis_index("shard") * local_rows + jnp.arange(local_rows, dtype=jnp.int32)
    grad_live = jnp.where((positions < live_count)[:, None], out_grad, jnp.zeros_like(out_grad))
    query_head, key_head, value_head = (
        lax.all_to_all(queries, "shard", split_axis=1, concat_axis=0, tiled=True),
        lax.all_to_all(keys_in, "shard", split_axis=1, concat_axis=0, tiled=True),
        lax.all_to_all(values, "shard", split_axis=1, concat_axis=0, tiled=True),
    )
    row_count, width_all = query_head.shape
    head_count = width_all // HDIM
    block_count = row_count // BLOCK
    score_scale = 1.0 / math.sqrt(HDIM)
    query_blk, key_blk, value_blk, probs = attend_listed(
        query_head, key_head, value_head, block_ids, live_count
    )
    prob_bf = probs.astype(jnp.bfloat16)
    heads_out = (
        jnp.einsum("bhqk,bkhd->bqhd", prob_bf, value_blk, preferred_element_type=jnp.float32)
        .reshape(row_count, width_all)
        .astype(jnp.bfloat16)
    )
    row_piece = lax.all_gather(grad_live, "shard", axis=0, tiled=True)
    acc_now = jnp.einsum("rw,ro->wo", heads_out, row_piece, preferred_element_type=jnp.float32)
    product = jnp.einsum("ro,wo->rw", row_piece, out_weight, preferred_element_type=jnp.float32)
    grad_o = product.astype(jnp.bfloat16).reshape(block_count, BLOCK, head_count, HDIM)
    grad_prob = jnp.einsum("bqhd,bkhd->bhqk", grad_o, value_blk, preferred_element_type=jnp.float32)
    row_delta = jnp.sum(probs * grad_prob, axis=-1, keepdims=True)
    dscore = (probs * (grad_prob - row_delta) * score_scale).astype(jnp.bfloat16)
    grad_query = (
        jnp.einsum("bhqk,bkhd->bqhd", dscore, key_blk, preferred_element_type=jnp.float32)
        .reshape(row_count, width_all)
        .astype(jnp.bfloat16)
    )
    onehot = (
        block_ids[:, :, None] == jnp.arange(block_count, dtype=jnp.int32)[None, None, :]
    ).astype(jnp.float32)
    key_parts = jnp.einsum(
        "bhqk,bqhd->bkhd", dscore, query_blk, preferred_element_type=jnp.float32
    ).reshape(block_count, NB, BLOCK, width_all)
    value_parts = jnp.einsum(
        "bhqk,bqhd->bkhd", prob_bf, grad_o, preferred_element_type=jnp.float32
    ).reshape(block_count, NB, BLOCK, width_all)
    grad_key = (
        jnp.einsum("bjc,bjrx->crx", onehot, key_parts, precision=lax.Precision.HIGHEST)
        .reshape(row_count, width_all)
        .astype(jnp.bfloat16)
    )
    grad_value = (
        jnp.einsum("bjc,bjrx->crx", onehot, value_parts, precision=lax.Precision.HIGHEST)
        .reshape(row_count, width_all)
        .astype(jnp.bfloat16)
    )
    query_back, key_back, value_back = (
        lax.all_to_all(grad_query, "shard", split_axis=0, concat_axis=1, tiled=True),
        lax.all_to_all(grad_key, "shard", split_axis=0, concat_axis=1, tiled=True),
        lax.all_to_all(grad_value, "shard", split_axis=0, concat_axis=1, tiled=True),
    )
    scene_total = lax.axis_size(DP)
    summed = lax.psum(acc_now, DP)
    grad_weight = (summed / scene_total).astype(jnp.bfloat16)
    return (query_back, key_back, value_back, grad_weight)


def body(queries, keys_in, values, out_grad, out_weight, block_lists, voxel_count):
    dense = block_lists.shape[1] == NB and queries.shape[0] == BLOCK
    if dense and lax.axis_size("shard") == 4 and lax.axis_size("chips") == 4:
        return dense_body(queries, keys_in, values, out_grad, out_weight, voxel_count)
    return listed_body(queries, keys_in, values, out_grad, out_weight, block_lists, voxel_count)


def solution(mesh):
    chips = mesh.shape["dp"] // 2
    mesh = jax.sharding.Mesh(mesh.devices.reshape(chips, 2, -1), ("chips", "core", "shard"))
    return jax.shard_map(
        body,
        mesh=mesh,
        in_specs=(
            P((*DP, "shard"), None),
            P((*DP, "shard"), None),
            P((*DP, "shard"), None),
            P((*DP, "shard"), None),
            P("shard", None),
            P(DP, None, None),
            P(DP),
        ),
        out_specs=(
            P((*DP, "shard"), None),
            P((*DP, "shard"), None),
            P((*DP, "shard"), None),
            P("shard", None),
        ),
        check_vma=False,
    )
```

profile of v0, /device:TPU:0, one launch (start us, length us, event | category | flops | bytes accessed | tf_op | source)
XLA Modules:
  0.0 121.5 jit_solution(2667599813870399836)
XLA Ops:
  0.6 0.0 copy-start
  0.6 3.1 %collective-permute-start.3 = (bf16[128,2048]{1,0:T(8,128)(2,1)}, bf16[128,2048]{1,0:T(8,128)(2,1)S(1)}, u32[]{:S(2)}, u32[]{:S(2)}) collective-permute-start(bf16[128,2048]{1,0:T(8,128)(2,1)} %grad_ref.1), channel_id=1, source_target_pairs={{0,1},{1,0},{2,3},{3,2},{4,5},{5,4},{6,7},{7,6},{8,9},{9,8},{10,11... | collective-permute-start | bytes 1572872 | tf_op jit(solution)/shard_map/ppermute | solution.py:40
  3.7 2.6 %collective-permute-start.1 = (bf16[128,2048]{1,0:T(8,128)(2,1)}, bf16[128,2048]{1,0:T(8,128)(2,1)S(1)}, u32[]{:S(2)}, u32[]{:S(2)}) collective-permute-start(bf16[128,2048]{1,0:T(8,128)(2,1)} %grad_ref.1), channel_id=1, source_target_pairs={{0,2},{1,3},{2,0},{3,1},{4,6},{5,7},{6,4},{7,5},{8,10},{9,11},{10,... | collective-permute-start | bytes 1572872 | tf_op jit(solution)/shard_map/ppermute | solution.py:40
  7.0 0.1 pad_add_fusion.meta
  7.0 0.0 copy-start.3
  7.1 1.0 copy-done.3
  8.1 1.0 copy-done.4
  9.1 1.0 copy-done.5
  10.2 1.0 copy-done.6
  11.2 1.1 pack_heads.1
  12.3 0.5 collective-permute-start
  12.8 15.0 %collective-permute-done.3.refs_1_ = bf16[128,2048]{1,0:T(8,128)(2,1)S(1)} collective-permute-done((bf16[128,2048]{1,0:T(8,128)(2,1)}, bf16[128,2048]{1,0:T(8,128)(2,1)S(1)}, u32[]{:S(2)}, u32[]{:S(2)}) %collective-permute-start.3) | collective-permute-done | bytes 524320 | tf_op jit(solution)/shard_map/ppermute | solution.py:40
  27.8 3.6 %collective-permute-start.4 = (bf16[3,128,384]{2,1,0:T(8,128)(2,1)S(1)}, bf16[3,128,384]{2,1,0:T(8,128)(2,1)S(1)}, u32[]{:S(2)}, u32[]{:S(2)}) collective-permute-start(bf16[3,128,384]{2,1,0:T(8,128)(2,1)S(1)} %get-tuple-element.50), channel_id=1, source_target_pairs={{0,3},{1,2},{2,1},{3,0},{4,7},{5,6},{6,5},{7,4},{8,11},{9,10},{10,... | collective-permute-start | bytes 884744 | tf_op jit(solution)/shard_map/ppermute | solution.py:40
  31.4 0.0 collective-permute-done.1.refs_2_
  31.4 0.0 collective-permute-start.2
  31.4 2.1 %collective-permute-start.7 = (bf16[64,2048]{1,0:T(8,128)(2,1)S(1)}, bf16[64,2048]{1,0:T(8,128)(2,1)S(1)}, u32[]{:S(2)}, u32[]{:S(2)}) collective-permute-start(bf16[64,2048]{1,0:T(8,128)(2,1)S(1)} %slice.8), channel_id=1, source_target_pairs={{0,1},{1,0},{2,3},{3,2},{4,5},{5,4},{6,7},{7,6},{8,9},{9,8},{10,11... | collective-permute-start | bytes 786440 | tf_op jit(solution)/shard_map/ppermute | solution.py:40
  33.5 0.0 copy-done
  33.5 1.9 %grad_attn.2.early_ref = bf16[384,512]{1,0:T(8,128)(2,1)S(1)} custom-call(s32[4]{0:T(128)S(1)} %pad_add_fusion.meta, bf16[128,2048]{1,0:T(8,128)(2,1)S(1)} %get-tuple-element.58.refs_0_, bf16[128,2048]{1,0:T(8,128)(2,1)S(1)} %collective-permute-done.3.refs_1_, bf16[128,2048]{1,0:T(8,128)(2,1)S(1)} %collective-permute-done.1.refs_2_, ...), custom_call_target="tpu_custom_call" | custom-call | bytes 1024 | tf_op jit(solution)/shard_map/grad_attn/pallas_call | solution.py:55
  35.4 8.7 %collective-permute-done.p1.near = bf16[3,128,512]{2,1,0:T(8,128)(2,1)S(1)} collective-permute-done((bf16[3,128,512]{2,1,0:T(8,128)(2,1)S(1)}, bf16[3,128,512]{2,1,0:T(8,128)(2,1)S(1)}, u32[]{:S(2)}, u32[]{:S(2)}) %collective-permute-start) | collective-permute-done | bytes 393248 | tf_op jit(solution)/shard_map/ppermute | solution.py:40
  44.1 0.1 collective-permute-start.8
  44.2 1.2 collective-permute-done.4.p3.far3a
  45.3 3.0 %collective-permute-start.6 = (bf16[3,128,128]{2,1,0:T(8,128)(2,1)S(1)}, bf16[3,128,128]{2,1,0:T(8,128)(2,1)S(1)}, u32[]{:S(2)}, u32[]{:S(2)}) collective-permute-start(bf16[3,128,128]{2,1,0:T(8,128)(2,1)S(1)} %get-tuple-element.55), channel_id=1, source_target_pairs={{0,3},{1,2},{2,1},{3,0},{4,7},{5,6},{6,5},{7,4},{8,11},{9,10},{10,... | collective-permute-start | bytes 294920 | tf_op jit(solution)/shard_map/ppermute | solution.py:40
  48.3 7.6 %collective-permute-done.2.p2.far2a = bf16[3,128,384]{2,1,0:T(8,128)(2,1)S(1)} collective-permute-done((bf16[3,128,384]{2,1,0:T(8,128)(2,1)S(1)}, bf16[3,128,384]{2,1,0:T(8,128)(2,1)S(1)}, u32[]{:S(2)}, u32[]{:S(2)}) %collective-permute-start.2) | collective-permute-done | bytes 294944 | tf_op jit(solution)/shard_map/ppermute | solution.py:40
  55.9 0.0 collective-permute-start.5
  55.9 3.4 %attend_forward.2 = (bf16[3,512,512]{2,1,0:T(8,128)(2,1)S(1)}, f32[3,1,512]{2,1,0:T(1,128)S(1)}, f32[384,512]{1,0:T(8,128)S(1)}, bf16[384,512]{1,0:T(8,128)(2,1)S(1)}) custom-call(s32[4]{0:T(128)S(1)} %pad_add_fusion.meta, bf16[3,128,512]{2,1,0:T(8,128)(2,1)S(1)} %get-tuple-element.45.p0.own, bf16[3,128,512]{2,1,0:T(8,128)(2,1)S(1)} %collective-permute-done.p1.near, ...), custom_call_target="tpu_custom_call" | custom-call | bytes 1024 | tf_op jit(solution)/shard_map/attend_forward/pallas_call | solution.py:55
  59.3 5.5 %collective-permute-done.6.p3.far3b = bf16[3,128,128]{2,1,0:T(8,128)(2,1)S(1)} collective-permute-done((bf16[3,128,128]{2,1,0:T(8,128)(2,1)S(1)}, bf16[3,128,128]{2,1,0:T(8,128)(2,1)S(1)}, u32[]{:S(2)}, u32[]{:S(2)}) %collective-permute-start.6) | collective-permute-done | bytes 98336 | tf_op jit(solution)/shard_map/ppermute | solution.py:40
  64.8 0.0 collective-permute-done.5.p2.far2b
  64.8 1.6 %attend_forward.3 = (bf16[1,512,512]{2,1,0:T(8,128)(2,1)S(1)}, f32[1,1,512]{2,1,0:T(1,128)S(1)}, f32[128,512]{1,0:T(8,128)S(1)}, bf16[128,512]{1,0:T(8,128)(2,1)S(1)}) custom-call(s32[4]{0:T(128)S(1)} %pad_add_fusion.meta, bf16[3,128,512]{2,1,0:T(8,128)(2,1)S(1)} %get-tuple-element.45.p0.own, bf16[3,128,512]{2,1,0:T(8,128)(2,1)S(1)} %collective-permute-done.p1.near, ...), custom_call_target="tpu_custom_call" | custom-call | bytes 1024 | tf_op jit(solution)/shard_map/attend_forward/pallas_call | solution.py:55
  66.5 0.0 collective-permute-done.7.refs_3_.refs_0_
  66.5 0.0 collective-permute-done.8.refs_4_.refs_1_
  66.5 2.4 %weight_halves.1 = (bf16[256,2048]{1,0:T(8,128)(2,1)S(1)}, f32[256,2048]{1,0:T(8,128)S(1)}) custom-call(s32[4]{0:T(128)S(1)} %pad_add_fusion.meta, bf16[384,512]{1,0:T(8,128)(2,1)S(1)} %get-tuple-element.64.heads_a, bf16[128,512]{1,0:T(8,128)(2,1)S(1)} %get-tuple-element.65.heads_b, bf16[128,2048]{1,0:T(8,128)(2,1)S(1)} %get-tuple-element.58.refs_0_, ...), custom_call_target="tpu_custom_call" | custom-call | bytes 1024 | tf_op jit(solution)/shard_map/weight_halves/pallas_call | solution.py:55
  68.9 0.0 copy-start.1
  68.9 0.1 collective-permute-start.9
  69.0 1.6 %grad_attn.3.late_ref = bf16[128,512]{1,0:T(8,128)(2,1)S(1)} custom-call(s32[4]{0:T(128)S(1)} %pad_add_fusion.meta, bf16[64,2048]{1,0:T(8,128)(2,1)S(1)} %collective-permute-done.7.refs_3_.refs_0_, bf16[64,2048]{1,0:T(8,128)(2,1)S(1)} %collective-permute-done.8.refs_4_.refs_1_, bf16[512,2048]{1,0:T(8,128)(2,1)S(1)} %copy-done), custom_call_target="tpu_custom_call" | custom-call | bytes 1024 | tf_op jit(solution)/shard_map/grad_attn/pallas_call | solution.py:55
  70.5 0.0 copy-done.1
  70.5 5.5 %attend_backward.1 = bf16[4,3,128,512]{3,2,1,0:T(8,128)(2,1)} custom-call(s32[4]{0:T(128)S(1)} %pad_add_fusion.meta, bf16[3,128,512]{2,1,0:T(8,128)(2,1)S(1)} %get-tuple-element.45.p0.own, bf16[3,128,512]{2,1,0:T(8,128)(2,1)S(1)} %collective-permute-done.p1.near, bf16[3,128,384]{2,1,0:T(8,128)(2,1)S(1)} %collective-permute-done.2.p2.far2a, ...), custom_call_target="tpu_custom_call" | custom-call | bytes 1024 | tf_op jit(solution)/shard_map/attend_backward/pallas_call | solution.py:55
  76.0 0.0 collective-permute-done.9.recv_ref
  76.0 4.1 %all-to-all-start = ((bf16[4,3,128,512]{3,2,1,0:T(8,128)(2,1)}), bf16[4,3,128,512]{3,2,1,0:T(8,128)(2,1)S(1)}, u32[]{:S(2)}, u32[]{:S(2)}) async-start(bf16[4,3,128,512]{3,2,1,0:T(8,128)(2,1)} %attend_backward.1), calls=%async_computation | async-start | bytes 3145728 | tf_op jit(solution)/shard_map/all_to_all | solution.py:342
  80.1 1.6 %copy-done.2 = f32[256,2048]{1,0:T(8,128)S(1)} copy-done((f32[256,2048]{1,0:T(8,128)S(1)}, f32[256,2048]{1,0:T(8,128)}, u32[]{:S(2)}) %copy-start.2) | copy-done | bytes 2097176
  81.7 0.2 add_parts.1
  81.9 1.6 %collective-permute-start.10 = (bf16[64,2048]{1,0:T(8,128)(2,1)S(1)}, bf16[64,2048]{1,0:T(8,128)(2,1)S(1)}, u32[]{:S(2)}, u32[]{:S(2)}) collective-permute-start(bf16[64,2048]{1,0:T(8,128)(2,1)S(1)} %get-tuple-element.82), channel_id=1, source_target_pairs={{0,8},{8,0},{16,24},{24,16},{1,9},{9,1},{17,25},{25,17},{2,10},{10... | collective-permute-start | bytes 786440 | tf_op jit(solution)/shard_map/ppermute | solution.py:40
  83.4 1.5 %collective-permute-start.11 = (bf16[64,2048]{1,0:T(8,128)(2,1)S(1)}, bf16[64,2048]{1,0:T(8,128)(2,1)S(1)}, u32[]{:S(2)}, u32[]{:S(2)}) collective-permute-start(bf16[64,2048]{1,0:T(8,128)(2,1)S(1)} %get-tuple-element.83), channel_id=1, source_target_pairs={{0,16},{8,24},{16,0},{24,8},{1,17},{9,25},{17,1},{25,9},{2,18},{10... | collective-permute-start | bytes 786440 | tf_op jit(solution)/shard_map/ppermute | solution.py:40
  84.9 0.5 collective-permute-start.12
  85.4 5.7 %collective-permute-done.10.r1 = bf16[64,2048]{1,0:T(8,128)(2,1)S(1)} collective-permute-done((bf16[64,2048]{1,0:T(8,128)(2,1)S(1)}, bf16[64,2048]{1,0:T(8,128)(2,1)S(1)}, u32[]{:S(2)}, u32[]{:S(2)}) %collective-permute-start.10) | collective-permute-done | bytes 262176 | tf_op jit(solution)/shard_map/ppermute | solution.py:40
  91.1 6.1 %collective-permute-done.11.r2 = bf16[64,2048]{1,0:T(8,128)(2,1)S(1)} collective-permute-done((bf16[64,2048]{1,0:T(8,128)(2,1)S(1)}, bf16[64,2048]{1,0:T(8,128)(2,1)S(1)}, u32[]{:S(2)}, u32[]{:S(2)}) %collective-permute-start.11) | collective-permute-done | bytes 262176 | tf_op jit(solution)/shard_map/ppermute | solution.py:40
  97.2 0.0 collective-permute-done.12.r3
  97.2 0.1 scene_mean.1.refs_0_
  97.3 1.6 %collective-permute-start.15 = (bf16[64,2048]{1,0:T(8,128)(2,1)S(1)}, bf16[64,2048]{1,0:T(8,128)(2,1)S(1)}, u32[]{:S(2)}, u32[]{:S(2)}) collective-permute-start(bf16[64,2048]{1,0:T(8,128)(2,1)S(1)} %scene_mean.1.refs_0_), channel_id=1, source_target_pairs={{0,24},{8,16},{16,8},{24,0},{1,25},{9,17},{17,9},{25,1},{2,26},{10... | collective-permute-start | bytes 786440 | tf_op jit(solution)/shard_map/ppermute | solution.py:40
  98.9 1.2 collective-permute-start.14
  100.1 0.8 collective-permute-start.13
  100.9 6.7 %collective-permute-done.15.refs_3_ = bf16[64,2048]{1,0:T(8,128)(2,1)S(1)} collective-permute-done((bf16[64,2048]{1,0:T(8,128)(2,1)S(1)}, bf16[64,2048]{1,0:T(8,128)(2,1)S(1)}, u32[]{:S(2)}, u32[]{:S(2)}) %collective-permute-start.15) | collective-permute-done | bytes 262176 | tf_op jit(solution)/shard_map/ppermute | solution.py:40
  107.6 0.0 collective-permute-start.19
  107.6 0.5 collective-permute-start.16
  108.1 3.2 %collective-permute-done.14.refs_2_ = bf16[64,2048]{1,0:T(8,128)(2,1)S(1)} collective-permute-done((bf16[64,2048]{1,0:T(8,128)(2,1)S(1)}, bf16[64,2048]{1,0:T(8,128)(2,1)S(1)}, u32[]{:S(2)}, u32[]{:S(2)}) %collective-permute-start.14) | collective-permute-done | bytes 262176 | tf_op jit(solution)/shard_map/ppermute | solution.py:40
  111.3 0.0 collective-permute-start.18
  111.3 0.0 collective-permute-done.13.refs_1_
  111.3 0.5 collective-permute-start.17
  111.8 5.9 %all-to-all-done.back_ref = bf16[4,3,128,512]{3,2,1,0:T(8,128)(2,1)S(1)} async-done(((bf16[4,3,128,512]{3,2,1,0:T(8,128)(2,1)}), bf16[4,3,128,512]{3,2,1,0:T(8,128)(2,1)S(1)}, u32[]{:S(2)}, u32[]{:S(2)}) %all-to-all-start) | async-done | bytes 1572896 | tf_op jit(solution)/shard_map/all_to_all | solution.py:342
  117.7 1.2 %join_heads.1 = (bf16[128,2048]{1,0:T(8,128)(2,1)}, bf16[128,2048]{1,0:T(8,128)(2,1)}, bf16[128,2048]{1,0:T(8,128)(2,1)}) custom-call(bf16[4,3,128,512]{3,2,1,0:T(8,128)(2,1)S(1)} %all-to-all-done.back_ref), custom_call_target="tpu_custom_call" | custom-call | bytes 1024 | tf_op jit(solution)/shard_map/join_heads/pallas_call | solution.py:300
  119.0 0.0 collective-permute-done.19.refs_7_
  119.0 0.0 collective-permute-done.16.refs_4_
  119.0 0.0 collective-permute-done.18.refs_6_
  119.0 0.0 collective-permute-done.17.refs_5_
  119.0 2.5 %join_weight.1 = bf16[512,2048]{1,0:T(8,128)(2,1)} custom-call(s32[4]{0:T(128)S(1)} %pad_add_fusion.meta, bf16[64,2048]{1,0:T(8,128)(2,1)S(1)} %scene_mean.1.refs_0_, bf16[64,2048]{1,0:T(8,128)(2,1)S(1)} %collective-permute-done.13.refs_1_, bf16[64,2048]{1,0:T(8,128)(2,1)S(1)} %collective-permute-done.14.refs_2_, ...), custom_call_target="tpu_custom_call" | custom-call | bytes 1024 | tf_op jit(solution)/shard_map/join_weight/pallas_call | solution.py:275
  (6 shorter events, 0.0 us)
Async XLA Ops:
  0.6 32.9 %copy-start = (bf16[512,2048]{1,0:T(8,128)(2,1)S(1)}, bf16[512,2048]{1,0:T(8,128)(2,1)}, u32[]{:S(2)}) copy-start(bf16[512,2048]{1,0:T(8,128)(2,1)} %refs_2_.1) | copy-start | bytes 6291460
  0.6 27.2 %collective-permute-start.3 = (bf16[128,2048]{1,0:T(8,128)(2,1)}, bf16[128,2048]{1,0:T(8,128)(2,1)S(1)}, u32[]{:S(2)}, u32[]{:S(2)}) collective-permute-start(bf16[128,2048]{1,0:T(8,128)(2,1)} %grad_ref.1), channel_id=1, source_target_pairs={{0,1},{1,0},{2,3},{3,2},{4,5},{5,4},{6,7},{7,6},{8,9},{9,8},{10,11... | collective-permute-start | bytes 1572872 | tf_op jit(solution)/shard_map/ppermute | solution.py:40
  3.7 27.7 %collective-permute-start.1 = (bf16[128,2048]{1,0:T(8,128)(2,1)}, bf16[128,2048]{1,0:T(8,128)(2,1)S(1)}, u32[]{:S(2)}, u32[]{:S(2)}) collective-permute-start(bf16[128,2048]{1,0:T(8,128)(2,1)} %grad_ref.1), channel_id=1, source_target_pairs={{0,2},{1,3},{2,0},{3,1},{4,6},{5,7},{6,4},{7,5},{8,10},{9,11},{10,... | collective-permute-start | bytes 1572872 | tf_op jit(solution)/shard_map/ppermute | solution.py:40
  7.0 1.0 copy-start.3
  8.1 1.0 copy-start.4
  9.1 1.0 copy-start.5
  10.2 1.0 copy-start.6
  12.3 31.8 %collective-permute-start = (bf16[3,128,512]{2,1,0:T(8,128)(2,1)S(1)}, bf16[3,128,512]{2,1,0:T(8,128)(2,1)S(1)}, u32[]{:S(2)}, u32[]{:S(2)}) collective-permute-start(bf16[3,128,512]{2,1,0:T(8,128)(2,1)S(1)} %get-tuple-element.46), channel_id=1, source_target_pairs={{0,1},{1,0},{2,3},{3,2},{4,5},{5,4},{6,7},{7,6},{8,9},{9,8},{10,11... | collective-permute-start | bytes 1179656 | tf_op jit(solution)/shard_map/ppermute | solution.py:40
  27.8 17.5 %collective-permute-start.4 = (bf16[3,128,384]{2,1,0:T(8,128)(2,1)S(1)}, bf16[3,128,384]{2,1,0:T(8,128)(2,1)S(1)}, u32[]{:S(2)}, u32[]{:S(2)}) collective-permute-start(bf16[3,128,384]{2,1,0:T(8,128)(2,1)S(1)} %get-tuple-element.50), channel_id=1, source_target_pairs={{0,3},{1,2},{2,1},{3,0},{4,7},{5,6},{6,5},{7,4},{8,11},{9,10},{10,... | collective-permute-start | bytes 884744 | tf_op jit(solution)/shard_map/ppermute | solution.py:40
  31.4 24.5 %collective-permute-start.2 = (bf16[3,128,384]{2,1,0:T(8,128)(2,1)S(1)}, bf16[3,128,384]{2,1,0:T(8,128)(2,1)S(1)}, u32[]{:S(2)}, u32[]{:S(2)}) collective-permute-start(bf16[3,128,384]{2,1,0:T(8,128)(2,1)S(1)} %get-tuple-element.48), channel_id=1, source_target_pairs={{0,2},{1,3},{2,0},{3,1},{4,6},{5,7},{6,4},{7,5},{8,10},{9,11},{10,... | collective-permute-start | bytes 884744 | tf_op jit(solution)/shard_map/ppermute | solution.py:40
  31.4 35.1 %collective-permute-start.7 = (bf16[64,2048]{1,0:T(8,128)(2,1)S(1)}, bf16[64,2048]{1,0:T(8,128)(2,1)S(1)}, u32[]{:S(2)}, u32[]{:S(2)}) collective-permute-start(bf16[64,2048]{1,0:T(8,128)(2,1)S(1)} %slice.8), channel_id=1, source_target_pairs={{0,1},{1,0},{2,3},{3,2},{4,5},{5,4},{6,7},{7,6},{8,9},{9,8},{10,11... | collective-permute-start | bytes 786440 | tf_op jit(solution)/shard_map/ppermute | solution.py:40
  44.1 22.4 %collective-permute-start.8 = (bf16[64,2048]{1,0:T(8,128)(2,1)S(1)}, bf16[64,2048]{1,0:T(8,128)(2,1)S(1)}, u32[]{:S(2)}, u32[]{:S(2)}) collective-permute-start(bf16[64,2048]{1,0:T(8,128)(2,1)S(1)} %slice.7), channel_id=1, source_target_pairs={{0,1},{1,0},{2,3},{3,2},{4,5},{5,4},{6,7},{7,6},{8,9},{9,8},{10,11... | collective-permute-start | bytes 786440 | tf_op jit(solution)/shard_map/ppermute | solution.py:40
  45.3 19.5 %collective-permute-start.6 = (bf16[3,128,128]{2,1,0:T(8,128)(2,1)S(1)}, bf16[3,128,128]{2,1,0:T(8,128)(2,1)S(1)}, u32[]{:S(2)}, u32[]{:S(2)}) collective-permute-start(bf16[3,128,128]{2,1,0:T(8,128)(2,1)S(1)} %get-tuple-element.55), channel_id=1, source_target_pairs={{0,3},{1,2},{2,1},{3,0},{4,7},{5,6},{6,5},{7,4},{8,11},{9,10},{10,... | collective-permute-start | bytes 294920 | tf_op jit(solution)/shard_map/ppermute | solution.py:40
  55.9 8.9 %collective-permute-start.5 = (bf16[3,128,128]{2,1,0:T(8,128)(2,1)S(1)}, bf16[3,128,128]{2,1,0:T(8,128)(2,1)S(1)}, u32[]{:S(2)}, u32[]{:S(2)}) collective-permute-start(bf16[3,128,128]{2,1,0:T(8,128)(2,1)S(1)} %get-tuple-element.53), channel_id=1, source_target_pairs={{0,2},{1,3},{2,0},{3,1},{4,6},{5,7},{6,4},{7,5},{8,10},{9,11},{10,... | collective-permute-start | bytes 294920 | tf_op jit(solution)/shard_map/ppermute | solution.py:40
  68.9 1.7 %copy-start.1 = (f32[256,2048]{1,0:T(8,128)}, f32[256,2048]{1,0:T(8,128)S(1)}, u32[]{:S(2)}) copy-start(f32[256,2048]{1,0:T(8,128)S(1)} %get-tuple-element.80.keep_ref) | copy-start | bytes 6291460
  68.9 7.1 %collective-permute-start.9 = (bf16[256,2048]{1,0:T(8,128)(2,1)S(1)}, bf16[256,2048]{1,0:T(8,128)(2,1)S(1)}, u32[]{:S(2)}, u32[]{:S(2)}) collective-permute-start(bf16[256,2048]{1,0:T(8,128)(2,1)S(1)} %get-tuple-element.66), channel_id=1, source_target_pairs={{0,4},{4,0},{1,5},{5,1},{2,6},{6,2},{3,7},{7,3},{8,12},{12,8},{9,1... | collective-permute-start | bytes 3145736 | tf_op jit(solution)/shard_map/ppermute | solution.py:40
  76.0 41.7 %all-to-all-start = ((bf16[4,3,128,512]{3,2,1,0:T(8,128)(2,1)}), bf16[4,3,128,512]{3,2,1,0:T(8,128)(2,1)S(1)}, u32[]{:S(2)}, u32[]{:S(2)}) async-start(bf16[4,3,128,512]{3,2,1,0:T(8,128)(2,1)} %attend_backward.1), calls=%async_computation | async-start | bytes 3145728 | tf_op jit(solution)/shard_map/all_to_all | solution.py:342
  80.1 1.6 %copy-start.2 = (f32[256,2048]{1,0:T(8,128)S(1)}, f32[256,2048]{1,0:T(8,128)}, u32[]{:S(2)}) copy-start(f32[256,2048]{1,0:T(8,128)} %copy-done.1) | copy-start | bytes 6291460
  81.9 9.2 %collective-permute-start.10 = (bf16[64,2048]{1,0:T(8,128)(2,1)S(1)}, bf16[64,2048]{1,0:T(8,128)(2,1)S(1)}, u32[]{:S(2)}, u32[]{:S(2)}) collective-permute-start(bf16[64,2048]{1,0:T(8,128)(2,1)S(1)} %get-tuple-element.82), channel_id=1, source_target_pairs={{0,8},{8,0},{16,24},{24,16},{1,9},{9,1},{17,25},{25,17},{2,10},{10... | collective-permute-start | bytes 786440 | tf_op jit(solution)/shard_map/ppermute | solution.py:40
  83.4 13.8 %collective-permute-start.11 = (bf16[64,2048]{1,0:T(8,128)(2,1)S(1)}, bf16[64,2048]{1,0:T(8,128)(2,1)S(1)}, u32[]{:S(2)}, u32[]{:S(2)}) collective-permute-start(bf16[64,2048]{1,0:T(8,128)(2,1)S(1)} %get-tuple-element.83), channel_id=1, source_target_pairs={{0,16},{8,24},{16,0},{24,8},{1,17},{9,25},{17,1},{25,9},{2,18},{10... | collective-permute-start | bytes 786440 | tf_op jit(solution)/shard_map/ppermute | solution.py:40
  84.9 12.2 %collective-permute-start.12 = (bf16[64,2048]{1,0:T(8,128)(2,1)S(1)}, bf16[64,2048]{1,0:T(8,128)(2,1)S(1)}, u32[]{:S(2)}, u32[]{:S(2)}) collective-permute-start(bf16[64,2048]{1,0:T(8,128)(2,1)S(1)} %get-tuple-element.84), channel_id=1, source_target_pairs={{0,24},{8,16},{16,8},{24,0},{1,25},{9,17},{17,9},{25,1},{2,26},{10... | collective-permute-start | bytes 786440 | tf_op jit(solution)/shard_map/ppermute | solution.py:40
  97.3 10.2 %collective-permute-start.15 = (bf16[64,2048]{1,0:T(8,128)(2,1)S(1)}, bf16[64,2048]{1,0:T(8,128)(2,1)S(1)}, u32[]{:S(2)}, u32[]{:S(2)}) collective-permute-start(bf16[64,2048]{1,0:T(8,128)(2,1)S(1)} %scene_mean.1.refs_0_), channel_id=1, source_target_pairs={{0,24},{8,16},{16,8},{24,0},{1,25},{9,17},{17,9},{25,1},{2,26},{10... | collective-permute-start | bytes 786440 | tf_op jit(solution)/shard_map/ppermute | solution.py:40
  98.9 12.4 %collective-permute-start.14 = (bf16[64,2048]{1,0:T(8,128)(2,1)S(1)}, bf16[64,2048]{1,0:T(8,128)(2,1)S(1)}, u32[]{:S(2)}, u32[]{:S(2)}) collective-permute-start(bf16[64,2048]{1,0:T(8,128)(2,1)S(1)} %scene_mean.1.refs_0_), channel_id=1, source_target_pairs={{0,16},{8,24},{16,0},{24,8},{1,17},{9,25},{17,1},{25,9},{2,18},{10... | collective-permute-start | bytes 786440 | tf_op jit(solution)/shard_map/ppermute | solution.py:40
  100.1 11.2 %collective-permute-start.13 = (bf16[64,2048]{1,0:T(8,128)(2,1)S(1)}, bf16[64,2048]{1,0:T(8,128)(2,1)S(1)}, u32[]{:S(2)}, u32[]{:S(2)}) collective-permute-start(bf16[64,2048]{1,0:T(8,128)(2,1)S(1)} %scene_mean.1.refs_0_), channel_id=1, source_target_pairs={{0,8},{8,0},{16,24},{24,16},{1,9},{9,1},{17,25},{25,17},{2,10},{10... | collective-permute-start | bytes 786440 | tf_op jit(solution)/shard_map/ppermute | solution.py:40
  107.6 11.4 %collective-permute-start.19 = (bf16[64,2048]{1,0:T(8,128)(2,1)S(1)}, bf16[64,2048]{1,0:T(8,128)(2,1)S(1)}, u32[]{:S(2)}, u32[]{:S(2)}) collective-permute-start(bf16[64,2048]{1,0:T(8,128)(2,1)S(1)} %collective-permute-done.15.refs_3_), channel_id=1, source_target_pairs={{0,4},{4,0},{1,5},{5,1},{2,6},{6,2},{3,7},{7,3},{8,12},{12,8},{9,1... | collective-permute-start | bytes 786440 | tf_op jit(solution)/shard_map/ppermute | solution.py:40
  107.6 11.4 %collective-permute-start.16 = (bf16[64,2048]{1,0:T(8,128)(2,1)S(1)}, bf16[64,2048]{1,0:T(8,128)(2,1)S(1)}, u32[]{:S(2)}, u32[]{:S(2)}) collective-permute-start(bf16[64,2048]{1,0:T(8,128)(2,1)S(1)} %scene_mean.1.refs_0_), channel_id=1, source_target_pairs={{0,4},{4,0},{1,5},{5,1},{2,6},{6,2},{3,7},{7,3},{8,12},{12,8},{9,1... | collective-permute-start | bytes 786440 | tf_op jit(solution)/shard_map/ppermute | solution.py:40
  111.3 7.7 %collective-permute-start.18 = (bf16[64,2048]{1,0:T(8,128)(2,1)S(1)}, bf16[64,2048]{1,0:T(8,128)(2,1)S(1)}, u32[]{:S(2)}, u32[]{:S(2)}) collective-permute-start(bf16[64,2048]{1,0:T(8,128)(2,1)S(1)} %collective-permute-done.14.refs_2_), channel_id=1, source_target_pairs={{0,4},{4,0},{1,5},{5,1},{2,6},{6,2},{3,7},{7,3},{8,12},{12,8},{9,1... | collective-permute-start | bytes 786440 | tf_op jit(solution)/shard_map/ppermute | solution.py:40
  111.3 7.7 %collective-permute-start.17 = (bf16[64,2048]{1,0:T(8,128)(2,1)S(1)}, bf16[64,2048]{1,0:T(8,128)(2,1)}, u32[]{:S(2)}, u32[]{:S(2)}) collective-permute-start(bf16[64,2048]{1,0:T(8,128)(2,1)S(1)} %collective-permute-done.13.refs_1_), channel_id=1, source_target_pairs={{0,4},{4,0},{1,5},{5,1},{2,6},{6,2},{3,7},{7,3},{8,12},{12,8},{9,1... | collective-permute-start | bytes 786440 | tf_op jit(solution)/shard_map/ppermute | solution.py:40
where the time goes:
time: 122 us
  waiting for transfers between devices  65.6 us (54%)
  starting transfers between devices  27.2 us (22%)
  Pallas kernels  21.4 us (18%)
  local copies, waits for them, and re-layouts  5.8 us (5%)
  between operations  1.46 us (1%)
    ppermute x20, waiting for transfers between devices, swap(): return lax.ppermute(x, axis, [(i, i ^ flip) for i in range(size)])  59.7 us
    ppermute x20, starting transfers between devices, swap(): return lax.ppermute(x, axis, [(i, i ^ flip) for i in range(size)])  23.1 us
    pallas_call x8, Pallas kernels, whole(): pl.pallas_call(kernel, out_shape=out_shape, in_specs=[pl.BlockSpec(memory...  16.5 us
    all_to_all x1, waiting for transfers between devices, dense_body(): lax.all_to_all(after(back, recv), 'shard', split_axis=0, concat_axis=0, t...  5.91 us
    unnamed x14, local copies, waits for them, and re-layouts  5.77 us
    all_to_all x1, starting transfers between devices, dense_body(): lax.all_to_all(after(back, recv), 'shard', split_axis=0, concat_axis=0, t...  4.12 us
    pallas_call x1, Pallas kernels, join_weight(): pl.pallas_call(join_weight_kernel, out_shape=sds((8 * size, outw), bf16),...  2.54 us
  transfers between devices with their start and end apart: 21, of which 10 were waited for; matrix products, arithmetic and copies ran while one was open for 0% of the time, Pallas kernels for 14%

commit v1 on v0

--- a/solution.py
+++ b/solution.py
@@ -165,8 +165,8 @@
     return whole(kernel, shapes, (meta, *pieces), "attend_forward", 1, 8, scratch)
 
 
-def backward_kernel(meta, own, near, far2a, far3a, far2b, far3b, early_ref, late_ref, *refs):
-    saved, back_ref, backs = (refs[:3], refs[3:6]), refs[6], refs[7:]
+def backward_kernel(own, near, far2a, far3a, far2b, far3b, early_ref, late_ref, *refs):
+    saved, backs = (refs[:3], refs[3:6]), refs[6:]
     rows = own.shape[1]
     total = 4 * rows
     tile = 2 * rows
@@ -196,14 +196,11 @@
             mine = slice(k * rows, (k + 1) * rows)
             backs[k][1, :, cols] = grad_key[mine].astype(bf16)
             backs[k][2, :, cols] = grad_value[mine].astype(bf16)
-    for k, ref in enumerate(backs):
-        back_ref[meta[Z] ^ k] = ref[...]
-
-
-def backward(meta, pieces, grads, saved):
-    shape = sds((4, *pieces[0].shape), bf16)
-    scratch = [pltpu.VMEM(pieces[0].shape, bf16)] * 4
-    return whole(backward_kernel, shape, (meta, *pieces, *grads, *saved), "attend_backward", 1, 8, scratch)
+
+
+def backward(pieces, grads, saved):
+    shapes = [sds(pieces[0].shape, bf16)] * 4
+    return whole(backward_kernel, shapes, (*pieces, *grads, *saved), "attend_backward", 0, 8)
 
 
 LINE = HDIM // 8
@@ -259,54 +256,59 @@
     return whole(functools.partial(total_kernel, scale), sds(own.shape, bf16), (own, *recvs), "scene_mean")
 
 
-def join_weight_kernel(meta, *refs):
-    *parts, out_ref, sems = refs
+def join_weight_kernel(first, count, meta, *refs):
+    parts, out_ref, sems = refs[:count], refs[-2], refs[-1]
     copies = []
-    for n, ref in enumerate(parts):
+    for p, ref in enumerate(parts, first):
         for h in range(ref.shape[0] // LINE):
-            line = out_ref.at[line_at(meta, h, n // 4, n % 4), :]
+            line = out_ref.at[line_at(meta, h, p // 4, p % 4), :]
             part = ref.at[pl.ds(h * LINE, LINE), :]
             copies.append(pltpu.make_async_copy(part, line, sems.at[len(copies)]))
     run_all(copies)
 
 
-def join_weight(meta, parts):
+def join_weight(meta, parts, first=0, out=None):
     size, outw = parts[0].shape
+    more = () if out is None else (out,)
     return pl.pallas_call(
-        join_weight_kernel,
+        functools.partial(join_weight_kernel, first, len(parts)),
         out_shape=sds((8 * size, outw), bf16),
-        in_specs=[pl.BlockSpec(memory_space=pltpu.SMEM)] + [pl.BlockSpec(memory_space=pltpu.VMEM)] * 8,
+        in_specs=[pl.BlockSpec(memory_space=pltpu.SMEM)]
+        + [pl.BlockSpec(memory_space=pltpu.VMEM)] * len(parts)
+        + [pl.BlockSpec(memory_space=pl.ANY)] * len(more),
         out_specs=pl.BlockSpec(memory_space=pl.ANY),
-        scratch_shapes=[pltpu.SemaphoreType.DMA((8 * size // LINE,))],
+        scratch_shapes=[pltpu.SemaphoreType.DMA((len(parts) * size // LINE,))],
+        input_output_aliases={1 + len(parts): 0} if more else {},
         compiler_params=params(),
         cost_estimate=NO_COST,
         name="join_weight",
-    )(meta, *parts)
-
-
-def join_kernel(back_ref, *refs):
-    *outs, sems = refs
-    width = back_ref.shape[3]
+    )(meta, *parts, *more)
+
+
+def join_kernel(meta, *refs):
+    *pieces, sems = refs
+    pieces, outs = pieces[:4], pieces[4:]
+    width = pieces[0].shape[2]
     copies = []
-    for j in range(4):
+    for k, ref in enumerate(pieces):
+        start = pl.multiple_of((meta[Z] ^ k) * width, 128)
         for i, out_ref in enumerate(outs):
-            cols = out_ref.at[:, pl.ds(j * width, width)]
-            copies.append(pltpu.make_async_copy(back_ref.at[j, i], cols, sems.at[len(copies)]))
+            copies.append(pltpu.make_async_copy(ref.at[i], out_ref.at[:, pl.ds(start, width)], sems.at[3 * k + i]))
     run_all(copies)
 
 
-def join(back):
-    _, _, rows, width = back.shape
+def join(meta, pieces):
+    _, rows, width = pieces[0].shape
     return pl.pallas_call(
         join_kernel,
         out_shape=[sds((rows, 4 * width), bf16)] * 3,
-        in_specs=[pl.BlockSpec(memory_space=pltpu.VMEM)],
+        in_specs=[pl.BlockSpec(memory_space=pltpu.SMEM)] + [pl.BlockSpec(memory_space=pltpu.VMEM)] * 4,
         out_specs=[pl.BlockSpec(memory_space=pl.ANY)] * 3,
         scratch_shapes=[pltpu.SemaphoreType.DMA((12,))],
         compiler_params=params(),
         cost_estimate=NO_COST,
         name="join_heads",
-    )(back)
+    )(meta, *pieces)
 
 
 def dense_body(queries, keys_in, values, out_grad, out_weight, voxel_count):
@@ -338,17 +340,17 @@
     recv = swap(out, "core", 2, 1)
     grad_late = grad_attn(meta, after(grads[3:], out), out_weight, 3 * BLOCK)
     pieces = (own, piece1, piece2a, piece3a, piece2b, piece3b)
-    back = backward(meta, pieces, (grad_early, grad_late), (*saved_a, *saved_b))
-    back_all = lax.all_to_all(after(back, recv), "shard", split_axis=0, concat_axis=0, tiled=True)
-
-    own_part, *sends = add_parts(after(keep, back), recv)
+    own0, *backs = backward(pieces, (grad_early, grad_late), (*saved_a, *saved_b))
+    own_part, *sends = add_parts(after(keep, own0), recv)
     recvs = [swap(x, "chips", 4, j + 1) for j, x in enumerate(sends)]
-    done = total_of(own_part, recvs, 1.0 / 8)
+    back1 = send(backs[0], 1)
+    back2, back3 = send(backs[1], 2), send(backs[2], 3, recvs[0])
+    done = total_of(after(own_part, back1), recvs, 1.0 / 8)
     near = [done] + [swap(done, "chips", 4, j) for j in (1, 2, 3)]
+    weight = join_weight(meta, near)
+    weight, *near, back2, back3 = lax.optimization_barrier((weight, *near, back2, back3))
     far = [swap(x, "core", 2, 1) for x in near]
-    grads_in = join(back_all)
-    far[-1] = after(far[-1], grads_in[0])
-    return (*grads_in, join_weight(meta, near + far))
+    return (*join(meta, (own0, back1, back2, back3)), join_weight(meta, far, 4, weight))
 
 
 def attend_listed(queries, keys_in, values, block_ids, live_count):

time: 122 us -> 119 us (0.975)
  the two profiles are of different devices: /device:TPU:0 before, /device:TPU:11 now
where the time goes in v1:
time: 119 us; the launch traced here: 118 us
  waiting for transfers between devices  59.4 us (50%)
  starting transfers between devices  32.4 us (27%)
  Pallas kernels  21 us (18%)
  local copies, waits for them, and re-layouts  4.21 us (4%)
  between operations  1.45 us (1%)
    ppermute x23, waiting for transfers between devices, swap(): return lax.ppermute(x, axis, [(i, i ^ flip) for i in range(size)])  59.4 us
    ppermute x23, starting transfers between devices, swap(): return lax.ppermute(x, axis, [(i, i ^ flip) for i in range(size)])  32.4 us
    pallas_call x8, Pallas kernels, whole(): pl.pallas_call(kernel, out_shape=out_shape, in_specs=[pl.BlockSpec(memory...  14.8 us
    unnamed x10, local copies, waits for them, and re-layouts  4.17 us
    pallas_call x2, Pallas kernels, join_weight(): pl.pallas_call(functools.partial(join_weight_kernel, first, len(parts)),...  3.27 us
  transfers between devices with their start and end apart: 23, of which 11 were waited for; matrix products, arithmetic and copies ran while one was open for 0% of the time, Pallas kernels for 14%

profile of v1, /device:TPU:11, one launch (start us, length us, event | category | flops | bytes accessed | tf_op | source)
XLA Modules:
  0.0 118.5 jit_solution(2375906035056581785)
XLA Ops:
  0.6 0.2 collective-permute-start.3
  0.9 2.3 %collective-permute-start.1 = (bf16[128,2048]{1,0:T(8,128)(2,1)}, bf16[128,2048]{1,0:T(8,128)(2,1)S(1)}, u32[]{:S(2)}, u32[]{:S(2)}) collective-permute-start(bf16[128,2048]{1,0:T(8,128)(2,1)} %grad_ref.1), channel_id=1, source_target_pairs={{0,2},{1,3},{2,0},{3,1},{4,6},{5,7},{6,4},{7,5},{8,10},{9,11},{10,... | collective-permute-start | bytes 1572872 | tf_op jit(solution)/shard_map/ppermute | solution.py:40
  3.8 0.1 pad_add_fusion.meta
  3.9 1.0 copy-done.1
  5.0 1.0 copy-done.2
  6.0 1.0 copy-done.3
  7.0 1.0 copy-done.4
  8.1 1.1 pack_heads.1
  9.2 1.4 %collective-permute-start = (bf16[3,128,512]{2,1,0:T(8,128)(2,1)S(1)}, bf16[3,128,512]{2,1,0:T(8,128)(2,1)S(1)}, u32[]{:S(2)}, u32[]{:S(2)}) collective-permute-start(bf16[3,128,512]{2,1,0:T(8,128)(2,1)S(1)} %get-tuple-element.57), channel_id=1, source_target_pairs={{0,1},{1,0},{2,3},{3,2},{4,5},{5,4},{6,7},{7,6},{8,9},{9,8},{10,11... | collective-permute-start | bytes 1179656 | tf_op jit(solution)/shard_map/ppermute | solution.py:40
  10.5 12.4 %collective-permute-done.3.refs_1_ = bf16[128,2048]{1,0:T(8,128)(2,1)S(1)} collective-permute-done((bf16[128,2048]{1,0:T(8,128)(2,1)}, bf16[128,2048]{1,0:T(8,128)(2,1)S(1)}, u32[]{:S(2)}, u32[]{:S(2)}) %collective-permute-start.3) | collective-permute-done | bytes 524320 | tf_op jit(solution)/shard_map/ppermute | solution.py:40
  22.9 1.3 %collective-permute-start.4 = (bf16[3,128,384]{2,1,0:T(8,128)(2,1)S(1)}, bf16[3,128,384]{2,1,0:T(8,128)(2,1)S(1)}, u32[]{:S(2)}, u32[]{:S(2)}) collective-permute-start(bf16[3,128,384]{2,1,0:T(8,128)(2,1)S(1)} %get-tuple-element.61), channel_id=1, source_target_pairs={{0,3},{1,2},{2,1},{3,0},{4,7},{5,6},{6,5},{7,4},{8,11},{9,10},{10,... | collective-permute-start | bytes 884744 | tf_op jit(solution)/shard_map/ppermute | solution.py:40
  24.2 1.8 %collective-permute-done.1.refs_2_ = bf16[128,2048]{1,0:T(8,128)(2,1)S(1)} collective-permute-done((bf16[128,2048]{1,0:T(8,128)(2,1)}, bf16[128,2048]{1,0:T(8,128)(2,1)S(1)}, u32[]{:S(2)}, u32[]{:S(2)}) %collective-permute-start.1) | collective-permute-done | bytes 524320 | tf_op jit(solution)/shard_map/ppermute | solution.py:40
  26.0 1.1 collective-permute-start.2
  27.1 0.4 collective-permute-start.7
  27.4 0.0 copy-done
  27.4 1.9 %grad_attn.2.early_ref = bf16[384,512]{1,0:T(8,128)(2,1)S(1)} custom-call(s32[4]{0:T(128)S(1)} %pad_add_fusion.meta, bf16[128,2048]{1,0:T(8,128)(2,1)S(1)} %get-tuple-element.69.refs_0_, bf16[128,2048]{1,0:T(8,128)(2,1)S(1)} %collective-permute-done.3.refs_1_, bf16[128,2048]{1,0:T(8,128)(2,1)S(1)} %collective-permute-done.1.refs_2_, ...), custom_call_target="tpu_custom_call" | custom-call | bytes 1024 | tf_op jit(solution)/shard_map/grad_attn/pallas_call | solution.py:55
  29.3 4.1 %collective-permute-done.p1.near = bf16[3,128,512]{2,1,0:T(8,128)(2,1)S(1)} collective-permute-done((bf16[3,128,512]{2,1,0:T(8,128)(2,1)S(1)}, bf16[3,128,512]{2,1,0:T(8,128)(2,1)S(1)}, u32[]{:S(2)}, u32[]{:S(2)}) %collective-permute-start) | collective-permute-done | bytes 393248 | tf_op jit(solution)/shard_map/ppermute | solution.py:40
  33.4 0.4 collective-permute-start.8
  33.8 0.0 collective-permute-done.4.p3.far3a
  33.8 9.2 %collective-permute-start.6 = (bf16[3,128,128]{2,1,0:T(8,128)(2,1)S(1)}, bf16[3,128,128]{2,1,0:T(8,128)(2,1)S(1)}, u32[]{:S(2)}, u32[]{:S(2)}) collective-permute-start(bf16[3,128,128]{2,1,0:T(8,128)(2,1)S(1)} %get-tuple-element.66), channel_id=1, source_target_pairs={{0,3},{1,2},{2,1},{3,0},{4,7},{5,6},{6,5},{7,4},{8,11},{9,10},{10,... | collective-permute-start | bytes 294920 | tf_op jit(solution)/shard_map/ppermute | solution.py:40
  43.0 6.9 %collective-permute-done.2.p2.far2a = bf16[3,128,384]{2,1,0:T(8,128)(2,1)S(1)} collective-permute-done((bf16[3,128,384]{2,1,0:T(8,128)(2,1)S(1)}, bf16[3,128,384]{2,1,0:T(8,128)(2,1)S(1)}, u32[]{:S(2)}, u32[]{:S(2)}) %collective-permute-start.2) | collective-permute-done | bytes 294944 | tf_op jit(solution)/shard_map/ppermute | solution.py:40
  49.9 3.1 %collective-permute-start.5 = (bf16[3,128,128]{2,1,0:T(8,128)(2,1)S(1)}, bf16[3,128,128]{2,1,0:T(8,128)(2,1)S(1)}, u32[]{:S(2)}, u32[]{:S(2)}) collective-permute-start(bf16[3,128,128]{2,1,0:T(8,128)(2,1)S(1)} %get-tuple-element.64), channel_id=1, source_target_pairs={{0,2},{1,3},{2,0},{3,1},{4,6},{5,7},{6,4},{7,5},{8,10},{9,11},{10,... | collective-permute-start | bytes 294920 | tf_op jit(solution)/shard_map/ppermute | solution.py:40
  53.0 3.4 %attend_forward.2 = (bf16[3,512,512]{2,1,0:T(8,128)(2,1)S(1)}, f32[3,1,512]{2,1,0:T(1,128)S(1)}, f32[384,512]{1,0:T(8,128)S(1)}, bf16[384,512]{1,0:T(8,128)(2,1)S(1)}) custom-call(s32[4]{0:T(128)S(1)} %pad_add_fusion.meta, bf16[3,128,512]{2,1,0:T(8,128)(2,1)S(1)} %get-tuple-element.56.p0.own, bf16[3,128,512]{2,1,0:T(8,128)(2,1)S(1)} %collective-permute-done.p1.near, ...), custom_call_target="tpu_custom_call" | custom-call | bytes 1024 | tf_op jit(solution)/shard_map/attend_forward/pallas_call | solution.py:55
  56.4 0.0 collective-permute-done.6.p3.far3b
  56.4 5.9 %collective-permute-done.5.p2.far2b = bf16[3,128,128]{2,1,0:T(8,128)(2,1)S(1)} collective-permute-done((bf16[3,128,128]{2,1,0:T(8,128)(2,1)S(1)}, bf16[3,128,128]{2,1,0:T(8,128)(2,1)S(1)}, u32[]{:S(2)}, u32[]{:S(2)}) %collective-permute-start.5) | collective-permute-done | bytes 98336 | tf_op jit(solution)/shard_map/ppermute | solution.py:40
  62.3 1.6 %attend_forward.3 = (bf16[1,512,512]{2,1,0:T(8,128)(2,1)S(1)}, f32[1,1,512]{2,1,0:T(1,128)S(1)}, f32[128,512]{1,0:T(8,128)S(1)}, bf16[128,512]{1,0:T(8,128)(2,1)S(1)}) custom-call(s32[4]{0:T(128)S(1)} %pad_add_fusion.meta, bf16[3,128,512]{2,1,0:T(8,128)(2,1)S(1)} %get-tuple-element.56.p0.own, bf16[3,128,512]{2,1,0:T(8,128)(2,1)S(1)} %collective-permute-done.p1.near, ...), custom_call_target="tpu_custom_call" | custom-call | bytes 1024 | tf_op jit(solution)/shard_map/attend_forward/pallas_call | solution.py:55
  63.9 0.0 collective-permute-done.7.refs_3_.refs_0_
  63.9 0.0 collective-permute-done.8.refs_4_.refs_1_
  63.9 2.4 %weight_halves.1 = (bf16[256,2048]{1,0:T(8,128)(2,1)S(1)}, f32[256,2048]{1,0:T(8,128)S(1)}) custom-call(s32[4]{0:T(128)S(1)} %pad_add_fusion.meta, bf16[384,512]{1,0:T(8,128)(2,1)S(1)} %get-tuple-element.75.heads_a, bf16[128,512]{1,0:T(8,128)(2,1)S(1)} %get-tuple-element.76.heads_b, bf16[128,2048]{1,0:T(8,128)(2,1)S(1)} %get-tuple-element.69.refs_0_, ...), custom_call_target="tpu_custom_call" | custom-call | bytes 1024 | tf_op jit(solution)/shard_map/weight_halves/pallas_call | solution.py:55
  66.3 1.9 %collective-permute-start.10 = (bf16[256,2048]{1,0:T(8,128)(2,1)S(1)}, bf16[256,2048]{1,0:T(8,128)(2,1)S(1)}, u32[]{:S(2)}, u32[]{:S(2)}) collective-permute-start(bf16[256,2048]{1,0:T(8,128)(2,1)S(1)} %get-tuple-element.77), channel_id=1, source_target_pairs={{0,4},{4,0},{1,5},{5,1},{2,6},{6,2},{3,7},{7,3},{8,12},{12,8},{9,1... | collective-permute-start | bytes 3145736 | tf_op jit(solution)/shard_map/ppermute | solution.py:40
  68.2 1.6 %grad_attn.3.late_ref = bf16[128,512]{1,0:T(8,128)(2,1)S(1)} custom-call(s32[4]{0:T(128)S(1)} %pad_add_fusion.meta, bf16[64,2048]{1,0:T(8,128)(2,1)S(1)} %collective-permute-done.7.refs_3_.refs_0_, bf16[64,2048]{1,0:T(8,128)(2,1)S(1)} %collective-permute-done.8.refs_4_.refs_1_, bf16[512,2048]{1,0:T(8,128)(2,1)S(1)} %copy-done), custom_call_target="tpu_custom_call" | custom-call | bytes 1024 | tf_op jit(solution)/shard_map/grad_attn/pallas_call | solution.py:55
  69.8 3.6 %attend_backward.1 = (bf16[3,128,512]{2,1,0:T(8,128)(2,1)S(1)}, bf16[3,128,512]{2,1,0:T(8,128)(2,1)S(1)}, bf16[3,128,512]{2,1,0:T(8,128)(2,1)S(1)}, bf16[3,128,512]{2,1,0:T(8,128)(2,1)S(1)}) custom-call(bf16[3,128,512]{2,1,0:T(8,128)(2,1)S(1)} %get-tuple-element.56.p0.own, bf16[3,128,512]{2,1,0:T(8,128)(2,1)S(1)} %collective-permute-done.p1.near, ...), custom_call_target="tpu_custom_call" | custom-call | bytes 1024 | tf_op jit(solution)/shard_map/attend_backward/pallas_call | solution.py:55
  73.4 0.2 collective-permute-start.9
  73.6 0.0 collective-permute-done.10.recv_ref
  73.6 0.3 add_parts.1
  73.9 0.3 collective-permute-start.11
  74.2 1.2 %collective-permute-start.12 = (bf16[64,2048]{1,0:T(8,128)(2,1)S(1)}, bf16[64,2048]{1,0:T(8,128)(2,1)S(1)}, u32[]{:S(2)}, u32[]{:S(2)}) collective-permute-start(bf16[64,2048]{1,0:T(8,128)(2,1)S(1)} %get-tuple-element.93), channel_id=1, source_target_pairs={{0,16},{8,24},{16,0},{24,8},{1,17},{9,25},{17,1},{25,9},{2,18},{10... | collective-permute-start | bytes 786440 | tf_op jit(solution)/shard_map/ppermute | solution.py:40
  75.4 1.2 collective-permute-start.13
  76.6 1.4 %collective-permute-start.17 = (bf16[3,128,512]{2,1,0:T(8,128)(2,1)S(1)}, bf16[3,128,512]{2,1,0:T(8,128)(2,1)S(1)}, u32[]{:S(2)}, u32[]{:S(2)}) collective-permute-start(bf16[3,128,512]{2,1,0:T(8,128)(2,1)S(1)} %get-tuple-element.95), channel_id=1, source_target_pairs={{0,2},{1,3},{2,0},{3,1},{4,6},{5,7},{6,4},{7,5},{8,10},{9,11},{10,... | collective-permute-start | bytes 1179656 | tf_op jit(solution)/shard_map/ppermute | solution.py:40
  78.0 3.5 %collective-permute-done.11.r1 = bf16[64,2048]{1,0:T(8,128)(2,1)S(1)} collective-permute-done((bf16[64,2048]{1,0:T(8,128)(2,1)S(1)}, bf16[64,2048]{1,0:T(8,128)(2,1)S(1)}, u32[]{:S(2)}, u32[]{:S(2)}) %collective-permute-start.11) | collective-permute-done | bytes 262176 | tf_op jit(solution)/shard_map/ppermute | solution.py:40
  81.5 1.7 %collective-permute-start.18 = (bf16[3,128,512]{2,1,0:T(8,128)(2,1)S(1)}, bf16[3,128,512]{2,1,0:T(8,128)(2,1)S(1)}, u32[]{:S(2)}, u32[]{:S(2)}) collective-permute-start(bf16[3,128,512]{2,1,0:T(8,128)(2,1)S(1)} %get-tuple-element.97), channel_id=1, source_target_pairs={{0,3},{1,2},{2,1},{3,0},{4,7},{5,6},{6,5},{7,4},{8,11},{9,10},{10,... | collective-permute-start | bytes 1179656 | tf_op jit(solution)/shard_map/ppermute | solution.py:40
  83.2 3.3 %collective-permute-done.9.refs_1_ = bf16[3,128,512]{2,1,0:T(8,128)(2,1)S(1)} collective-permute-done((bf16[3,128,512]{2,1,0:T(8,128)(2,1)S(1)}, bf16[3,128,512]{2,1,0:T(8,128)(2,1)S(1)}, u32[]{:S(2)}, u32[]{:S(2)}) %collective-permute-start.9) | collective-permute-done | bytes 393248 | tf_op jit(solution)/shard_map/ppermute | solution.py:40
  86.5 0.0 collective-permute-done.12.r2
  86.5 1.6 %collective-permute-done.13.r3 = bf16[64,2048]{1,0:T(8,128)(2,1)S(1)} collective-permute-done((bf16[64,2048]{1,0:T(8,128)(2,1)S(1)}, bf16[64,2048]{1,0:T(8,128)(2,1)S(1)}, u32[]{:S(2)}, u32[]{:S(2)}) %collective-permute-start.13) | collective-permute-done | bytes 262176 | tf_op jit(solution)/shard_map/ppermute | solution.py:40
  88.1 0.1 scene_mean.1.refs_0_
  88.3 1.2 %collective-permute-start.16 = (bf16[64,2048]{1,0:T(8,128)(2,1)S(1)}, bf16[64,2048]{1,0:T(8,128)(2,1)S(1)}, u32[]{:S(2)}, u32[]{:S(2)}) collective-permute-start(bf16[64,2048]{1,0:T(8,128)(2,1)S(1)} %scene_mean.1.refs_0_), channel_id=1, source_target_pairs={{0,24},{8,16},{16,8},{24,0},{1,25},{9,17},{17,9},{25,1},{2,26},{10... | collective-permute-start | bytes 786440 | tf_op jit(solution)/shard_map/ppermute | solution.py:40
  89.5 0.3 collective-permute-start.15
  89.8 1.2 collective-permute-start.14
  91.0 5.0 %collective-permute-done.16.refs_3_ = bf16[64,2048]{1,0:T(8,128)(2,1)S(1)} collective-permute-done((bf16[64,2048]{1,0:T(8,128)(2,1)S(1)}, bf16[64,2048]{1,0:T(8,128)(2,1)S(1)}, u32[]{:S(2)}, u32[]{:S(2)}) %collective-permute-start.16) | collective-permute-done | bytes 262176 | tf_op jit(solution)/shard_map/ppermute | solution.py:40
  95.9 7.1 %collective-permute-done.15.refs_2_ = bf16[64,2048]{1,0:T(8,128)(2,1)S(1)} collective-permute-done((bf16[64,2048]{1,0:T(8,128)(2,1)S(1)}, bf16[64,2048]{1,0:T(8,128)(2,1)S(1)}, u32[]{:S(2)}, u32[]{:S(2)}) %collective-permute-start.15) | collective-permute-done | bytes 262176 | tf_op jit(solution)/shard_map/ppermute | solution.py:40
  103.1 0.0 collective-permute-done.14.refs_1_
  103.1 1.6 %join_weight.2.refs_4_ = bf16[512,2048]{1,0:T(8,128)(2,1)} custom-call(s32[4]{0:T(128)S(1)} %pad_add_fusion.meta, bf16[64,2048]{1,0:T(8,128)(2,1)S(1)} %scene_mean.1.refs_0_, bf16[64,2048]{1,0:T(8,128)(2,1)S(1)} %collective-permute-done.14.refs_1_, bf16[64,2048]{1,0:T(8,128)(2,1)S(1)} %collective-permute-done.15.refs_2_, ...), custom_call_target="tpu_custom_call" | custom-call | bytes 1024 | tf_op jit(solution)/shard_map/join_weight/pallas_call | solution.py:273
  104.7 0.0 collective-permute-done.17.refs_2_
  104.7 7.8 %collective-permute-done.18.refs_3_ = bf16[3,128,512]{2,1,0:T(8,128)(2,1)S(1)} collective-permute-done((bf16[3,128,512]{2,1,0:T(8,128)(2,1)S(1)}, bf16[3,128,512]{2,1,0:T(8,128)(2,1)S(1)}, u32[]{:S(2)}, u32[]{:S(2)}) %collective-permute-start.18) | collective-permute-done | bytes 393248 | tf_op jit(solution)/shard_map/ppermute | solution.py:40
  112.5 2.0 %collective-permute-start.19 = (bf16[64,2048]{1,0:T(8,128)(2,1)S(1)}, bf16[64,2048]{1,0:T(8,128)(2,1)S(1)}, u32[]{:S(2)}, u32[]{:S(2)}) collective-permute-start(bf16[64,2048]{1,0:T(8,128)(2,1)S(1)} %scene_mean.1.refs_0_), channel_id=1, source_target_pairs={{0,4},{4,0},{1,5},{5,1},{2,6},{6,2},{3,7},{7,3},{8,12},{12,8},{9,1... | collective-permute-start | bytes 786440 | tf_op jit(solution)/shard_map/ppermute | solution.py:40
  114.5 0.0 collective-permute-start.20
  114.5 0.5 collective-permute-start.21
  115.0 0.0 collective-permute-start.22
  115.0 1.8 %join_heads.1 = (bf16[128,2048]{1,0:T(8,128)(2,1)}, bf16[128,2048]{1,0:T(8,128)(2,1)}, bf16[128,2048]{1,0:T(8,128)(2,1)}) custom-call(s32[4]{0:T(128)S(1)} %pad_add_fusion.meta, bf16[3,128,512]{2,1,0:T(8,128)(2,1)S(1)} %get-tuple-element.86.refs_0_, bf16[3,128,512]{2,1,0:T(8,128)(2,1)S(1)} %collective-permute-done.9.refs_1_, ...), custom_call_target="tpu_custom_call" | custom-call | bytes 1024 | tf_op jit(solution)/shard_map/join_heads/pallas_call | solution.py:302
  116.8 0.0 collective-permute-done.19.refs_0_
  116.8 0.0 collective-permute-done.20.refs_1_
  116.8 0.0 collective-permute-done.21.refs_2_
  116.8 0.0 collective-permute-done.22.refs_3_
  116.8 1.6 %join_weight.3 = bf16[512,2048]{1,0:T(8,128)(2,1)} custom-call(s32[4]{0:T(128)S(1)} %pad_add_fusion.meta, bf16[64,2048]{1,0:T(8,128)(2,1)S(1)} %collective-permute-done.19.refs_0_, bf16[64,2048]{1,0:T(8,128)(2,1)S(1)} %collective-permute-done.20.refs_1_, bf16[64,2048]{1,0:T(8,128)(2,1)S(1)} %collective-permute-done.21.refs_2_, ...), custom_call_target="tpu_custom_call", output_to_operand_aliasing={{}: (5, {})} | custom-call | bytes 1024 | tf_op jit(solution)/shard_map/join_weight/pallas_call | solution.py:273
  (7 shorter events, 0.0 us)
Async XLA Ops:
  0.6 26.8 %copy-start = (bf16[512,2048]{1,0:T(8,128)(2,1)S(1)}, bf16[512,2048]{1,0:T(8,128)(2,1)}, u32[]{:S(2)}) copy-start(bf16[512,2048]{1,0:T(8,128)(2,1)} %refs_2_.1) | copy-start | bytes 6291460
  0.6 22.2 %collective-permute-start.3 = (bf16[128,2048]{1,0:T(8,128)(2,1)}, bf16[128,2048]{1,0:T(8,128)(2,1)S(1)}, u32[]{:S(2)}, u32[]{:S(2)}) collective-permute-start(bf16[128,2048]{1,0:T(8,128)(2,1)} %grad_ref.1), channel_id=1, source_target_pairs={{0,1},{1,0},{2,3},{3,2},{4,5},{5,4},{6,7},{7,6},{8,9},{9,8},{10,11... | collective-permute-start | bytes 1572872 | tf_op jit(solution)/shard_map/ppermute | solution.py:40
  0.9 25.1 %collective-permute-start.1 = (bf16[128,2048]{1,0:T(8,128)(2,1)}, bf16[128,2048]{1,0:T(8,128)(2,1)S(1)}, u32[]{:S(2)}, u32[]{:S(2)}) collective-permute-start(bf16[128,2048]{1,0:T(8,128)(2,1)} %grad_ref.1), channel_id=1, source_target_pairs={{0,2},{1,3},{2,0},{3,1},{4,6},{5,7},{6,4},{7,5},{8,10},{9,11},{10,... | collective-permute-start | bytes 1572872 | tf_op jit(solution)/shard_map/ppermute | solution.py:40
  3.9 1.0 copy-start.1
  5.0 1.0 copy-start.2
  6.0 1.0 copy-start.3
  7.0 1.0 copy-start.4
  9.2 24.3 %collective-permute-start = (bf16[3,128,512]{2,1,0:T(8,128)(2,1)S(1)}, bf16[3,128,512]{2,1,0:T(8,128)(2,1)S(1)}, u32[]{:S(2)}, u32[]{:S(2)}) collective-permute-start(bf16[3,128,512]{2,1,0:T(8,128)(2,1)S(1)} %get-tuple-element.57), channel_id=1, source_target_pairs={{0,1},{1,0},{2,3},{3,2},{4,5},{5,4},{6,7},{7,6},{8,9},{9,8},{10,11... | collective-permute-start | bytes 1179656 | tf_op jit(solution)/shard_map/ppermute | solution.py:40
  22.9 10.9 %collective-permute-start.4 = (bf16[3,128,384]{2,1,0:T(8,128)(2,1)S(1)}, bf16[3,128,384]{2,1,0:T(8,128)(2,1)S(1)}, u32[]{:S(2)}, u32[]{:S(2)}) collective-permute-start(bf16[3,128,384]{2,1,0:T(8,128)(2,1)S(1)} %get-tuple-element.61), channel_id=1, source_target_pairs={{0,3},{1,2},{2,1},{3,0},{4,7},{5,6},{6,5},{7,4},{8,11},{9,10},{10,... | collective-permute-start | bytes 884744 | tf_op jit(solution)/shard_map/ppermute | solution.py:40
  26.0 23.9 %collective-permute-start.2 = (bf16[3,128,384]{2,1,0:T(8,128)(2,1)S(1)}, bf16[3,128,384]{2,1,0:T(8,128)(2,1)S(1)}, u32[]{:S(2)}, u32[]{:S(2)}) collective-permute-start(bf16[3,128,384]{2,1,0:T(8,128)(2,1)S(1)} %get-tuple-element.59), channel_id=1, source_target_pairs={{0,2},{1,3},{2,0},{3,1},{4,6},{5,7},{6,4},{7,5},{8,10},{9,11},{10,... | collective-permute-start | bytes 884744 | tf_op jit(solution)/shard_map/ppermute | solution.py:40
  27.1 36.8 %collective-permute-start.7 = (bf16[64,2048]{1,0:T(8,128)(2,1)S(1)}, bf16[64,2048]{1,0:T(8,128)(2,1)S(1)}, u32[]{:S(2)}, u32[]{:S(2)}) collective-permute-start(bf16[64,2048]{1,0:T(8,128)(2,1)S(1)} %slice.8), channel_id=1, source_target_pairs={{0,1},{1,0},{2,3},{3,2},{4,5},{5,4},{6,7},{7,6},{8,9},{9,8},{10,11... | collective-permute-start | bytes 786440 | tf_op jit(solution)/shard_map/ppermute | solution.py:40
  33.4 30.5 %collective-permute-start.8 = (bf16[64,2048]{1,0:T(8,128)(2,1)S(1)}, bf16[64,2048]{1,0:T(8,128)(2,1)S(1)}, u32[]{:S(2)}, u32[]{:S(2)}) collective-permute-start(bf16[64,2048]{1,0:T(8,128)(2,1)S(1)} %slice.7), channel_id=1, source_target_pairs={{0,1},{1,0},{2,3},{3,2},{4,5},{5,4},{6,7},{7,6},{8,9},{9,8},{10,11... | collective-permute-start | bytes 786440 | tf_op jit(solution)/shard_map/ppermute | solution.py:40
  33.8 22.6 %collective-permute-start.6 = (bf16[3,128,128]{2,1,0:T(8,128)(2,1)S(1)}, bf16[3,128,128]{2,1,0:T(8,128)(2,1)S(1)}, u32[]{:S(2)}, u32[]{:S(2)}) collective-permute-start(bf16[3,128,128]{2,1,0:T(8,128)(2,1)S(1)} %get-tuple-element.66), channel_id=1, source_target_pairs={{0,3},{1,2},{2,1},{3,0},{4,7},{5,6},{6,5},{7,4},{8,11},{9,10},{10,... | collective-permute-start | bytes 294920 | tf_op jit(solution)/shard_map/ppermute | solution.py:40
  49.9 12.4 %collective-permute-start.5 = (bf16[3,128,128]{2,1,0:T(8,128)(2,1)S(1)}, bf16[3,128,128]{2,1,0:T(8,128)(2,1)S(1)}, u32[]{:S(2)}, u32[]{:S(2)}) collective-permute-start(bf16[3,128,128]{2,1,0:T(8,128)(2,1)S(1)} %get-tuple-element.64), channel_id=1, source_target_pairs={{0,2},{1,3},{2,0},{3,1},{4,6},{5,7},{6,4},{7,5},{8,10},{9,11},{10,... | collective-permute-start | bytes 294920 | tf_op jit(solution)/shard_map/ppermute | solution.py:40
  66.3 7.3 %collective-permute-start.10 = (bf16[256,2048]{1,0:T(8,128)(2,1)S(1)}, bf16[256,2048]{1,0:T(8,128)(2,1)S(1)}, u32[]{:S(2)}, u32[]{:S(2)}) collective-permute-start(bf16[256,2048]{1,0:T(8,128)(2,1)S(1)} %get-tuple-element.77), channel_id=1, source_target_pairs={{0,4},{4,0},{1,5},{5,1},{2,6},{6,2},{3,7},{7,3},{8,12},{12,8},{9,1... | collective-permute-start | bytes 3145736 | tf_op jit(solution)/shard_map/ppermute | solution.py:40
  73.4 13.1 %collective-permute-start.9 = (bf16[3,128,512]{2,1,0:T(8,128)(2,1)S(1)}, bf16[3,128,512]{2,1,0:T(8,128)(2,1)S(1)}, u32[]{:S(2)}, u32[]{:S(2)}) collective-permute-start(bf16[3,128,512]{2,1,0:T(8,128)(2,1)S(1)} %get-tuple-element.87), channel_id=1, source_target_pairs={{0,1},{1,0},{2,3},{3,2},{4,5},{5,4},{6,7},{7,6},{8,9},{9,8},{10,11... | collective-permute-start | bytes 1179656 | tf_op jit(solution)/shard_map/ppermute | solution.py:40
  73.9 7.7 %collective-permute-start.11 = (bf16[64,2048]{1,0:T(8,128)(2,1)S(1)}, bf16[64,2048]{1,0:T(8,128)(2,1)S(1)}, u32[]{:S(2)}, u32[]{:S(2)}) collective-permute-start(bf16[64,2048]{1,0:T(8,128)(2,1)S(1)} %get-tuple-element.92), channel_id=1, source_target_pairs={{0,8},{8,0},{16,24},{24,16},{1,9},{9,1},{17,25},{25,17},{2,10},{10... | collective-permute-start | bytes 786440 | tf_op jit(solution)/shard_map/ppermute | solution.py:40
  74.2 12.3 %collective-permute-start.12 = (bf16[64,2048]{1,0:T(8,128)(2,1)S(1)}, bf16[64,2048]{1,0:T(8,128)(2,1)S(1)}, u32[]{:S(2)}, u32[]{:S(2)}) collective-permute-start(bf16[64,2048]{1,0:T(8,128)(2,1)S(1)} %get-tuple-element.93), channel_id=1, source_target_pairs={{0,16},{8,24},{16,0},{24,8},{1,17},{9,25},{17,1},{25,9},{2,18},{10... | collective-permute-start | bytes 786440 | tf_op jit(solution)/shard_map/ppermute | solution.py:40
  75.4 12.7 %collective-permute-start.13 = (bf16[64,2048]{1,0:T(8,128)(2,1)S(1)}, bf16[64,2048]{1,0:T(8,128)(2,1)S(1)}, u32[]{:S(2)}, u32[]{:S(2)}) collective-permute-start(bf16[64,2048]{1,0:T(8,128)(2,1)S(1)} %get-tuple-element.94), channel_id=1, source_target_pairs={{0,24},{8,16},{16,8},{24,0},{1,25},{9,17},{17,9},{25,1},{2,26},{10... | collective-permute-start | bytes 786440 | tf_op jit(solution)/shard_map/ppermute | solution.py:40
  76.6 28.1 %collective-permute-start.17 = (bf16[3,128,512]{2,1,0:T(8,128)(2,1)S(1)}, bf16[3,128,512]{2,1,0:T(8,128)(2,1)S(1)}, u32[]{:S(2)}, u32[]{:S(2)}) collective-permute-start(bf16[3,128,512]{2,1,0:T(8,128)(2,1)S(1)} %get-tuple-element.95), channel_id=1, source_target_pairs={{0,2},{1,3},{2,0},{3,1},{4,6},{5,7},{6,4},{7,5},{8,10},{9,11},{10,... | collective-permute-start | bytes 1179656 | tf_op jit(solution)/shard_map/ppermute | solution.py:40
  81.5 30.9 %collective-permute-start.18 = (bf16[3,128,512]{2,1,0:T(8,128)(2,1)S(1)}, bf16[3,128,512]{2,1,0:T(8,128)(2,1)S(1)}, u32[]{:S(2)}, u32[]{:S(2)}) collective-permute-start(bf16[3,128,512]{2,1,0:T(8,128)(2,1)S(1)} %get-tuple-element.97), channel_id=1, source_target_pairs={{0,3},{1,2},{2,1},{3,0},{4,7},{5,6},{6,5},{7,4},{8,11},{9,10},{10,... | collective-permute-start | bytes 1179656 | tf_op jit(solution)/shard_map/ppermute | solution.py:40
  88.3 7.7 %collective-permute-start.16 = (bf16[64,2048]{1,0:T(8,128)(2,1)S(1)}, bf16[64,2048]{1,0:T(8,128)(2,1)S(1)}, u32[]{:S(2)}, u32[]{:S(2)}) collective-permute-start(bf16[64,2048]{1,0:T(8,128)(2,1)S(1)} %scene_mean.1.refs_0_), channel_id=1, source_target_pairs={{0,24},{8,16},{16,8},{24,0},{1,25},{9,17},{17,9},{25,1},{2,26},{10... | collective-permute-start | bytes 786440 | tf_op jit(solution)/shard_map/ppermute | solution.py:40
  89.5 13.6 %collective-permute-start.15 = (bf16[64,2048]{1,0:T(8,128)(2,1)S(1)}, bf16[64,2048]{1,0:T(8,128)(2,1)S(1)}, u32[]{:S(2)}, u32[]{:S(2)}) collective-permute-start(bf16[64,2048]{1,0:T(8,128)(2,1)S(1)} %scene_mean.1.refs_0_), channel_id=1, source_target_pairs={{0,16},{8,24},{16,0},{24,8},{1,17},{9,25},{17,1},{25,9},{2,18},{10... | collective-permute-start | bytes 786440 | tf_op jit(solution)/shard_map/ppermute | solution.py:40
  89.8 13.3 %collective-permute-start.14 = (bf16[64,2048]{1,0:T(8,128)(2,1)S(1)}, bf16[64,2048]{1,0:T(8,128)(2,1)S(1)}, u32[]{:S(2)}, u32[]{:S(2)}) collective-permute-start(bf16[64,2048]{1,0:T(8,128)(2,1)S(1)} %scene_mean.1.refs_0_), channel_id=1, source_target_pairs={{0,8},{8,0},{16,24},{24,16},{1,9},{9,1},{17,25},{25,17},{2,10},{10... | collective-permute-start | bytes 786440 | tf_op jit(solution)/shard_map/ppermute | solution.py:40
  112.5 4.3 %collective-permute-start.19 = (bf16[64,2048]{1,0:T(8,128)(2,1)S(1)}, bf16[64,2048]{1,0:T(8,128)(2,1)S(1)}, u32[]{:S(2)}, u32[]{:S(2)}) collective-permute-start(bf16[64,2048]{1,0:T(8,128)(2,1)S(1)} %scene_mean.1.refs_0_), channel_id=1, source_target_pairs={{0,4},{4,0},{1,5},{5,1},{2,6},{6,2},{3,7},{7,3},{8,12},{12,8},{9,1... | collective-permute-start | bytes 786440 | tf_op jit(solution)/shard_map/ppermute | solution.py:40
  114.5 2.3 %collective-permute-start.20 = (bf16[64,2048]{1,0:T(8,128)(2,1)S(1)}, bf16[64,2048]{1,0:T(8,128)(2,1)S(1)}, u32[]{:S(2)}, u32[]{:S(2)}) collective-permute-start(bf16[64,2048]{1,0:T(8,128)(2,1)S(1)} %collective-permute-done.14.refs_1_), channel_id=1, source_target_pairs={{0,4},{4,0},{1,5},{5,1},{2,6},{6,2},{3,7},{7,3},{8,12},{12,8},{9,1... | collective-permute-start | bytes 786440 | tf_op jit(solution)/shard_map/ppermute | solution.py:40
  114.5 2.3 %collective-permute-start.21 = (bf16[64,2048]{1,0:T(8,128)(2,1)S(1)}, bf16[64,2048]{1,0:T(8,128)(2,1)S(1)}, u32[]{:S(2)}, u32[]{:S(2)}) collective-permute-start(bf16[64,2048]{1,0:T(8,128)(2,1)S(1)} %collective-permute-done.15.refs_2_), channel_id=1, source_target_pairs={{0,4},{4,0},{1,5},{5,1},{2,6},{6,2},{3,7},{7,3},{8,12},{12,8},{9,1... | collective-permute-start | bytes 786440 | tf_op jit(solution)/shard_map/ppermute | solution.py:40
  115.0 1.8 %collective-permute-start.22 = (bf16[64,2048]{1,0:T(8,128)(2,1)S(1)}, bf16[64,2048]{1,0:T(8,128)(2,1)S(1)}, u32[]{:S(2)}, u32[]{:S(2)}) collective-permute-start(bf16[64,2048]{1,0:T(8,128)(2,1)S(1)} %collective-permute-done.16.refs_3_), channel_id=1, source_target_pairs={{0,4},{4,0},{1,5},{5,1},{2,6},{6,2},{3,7},{7,3},{8,12},{12,8},{9,1... | collective-permute-start | bytes 786440 | tf_op jit(solution)/shard_map/ppermute | solution.py:40
